TPU v7x, 512 devices: a whole 4x8x8 slice. The times are simulated.
512 devices in a mesh: dp: 16 (over z, core), vocab: 32 (over y, x).
Axes of the slice: x: 4, y: 8, z: 8, core: 2. Of those that a mesh axis runs over, the one named last changes fastest.
Arguments:
- student_hidden: bfloat16 [480, 2048], P('dp', 'vocab'), may hold values from -8 to 8
- teacher_hidden: bfloat16 [480, 4096], P('dp', 'vocab'), may hold values from -8 to 8
- student_head: bfloat16 [128000, 2048], P(('dp', 'vocab')), may hold values from -0.35 to 0.35
- teacher_head: bfloat16 [128000, 4096], P(('dp', 'vocab')), may hold values from -0.35 to 0.35
Outputs:
- loss: float32 [], replicated
- hidden_grad: float32 [480, 2048], P('dp', 'vocab')
- head_grad: bfloat16 [128000, 2048], P(('dp', 'vocab'))
All inputs are finite; a program needn't handle non-finite values.
Results may differ from a plain program's by a relative error of at most 0.0046.
Values may be sent and summed in bfloat16 or wider, within the bound.
No kernel may reach another device: no remote copies, remote signals or barrier semaphores. Data moves between devices by JAX's collectives and lax.ppermute only.
A program may use at most 64 MiB of HBM per device.

v0:
```python
import jax
import jax.numpy as jnp
from jax import lax
from jax.sharding import PartitionSpec as P


def local(student_hidden, teacher_hidden, student_head, teacher_head):
    wide_s, wide_t = (
        lax.all_gather(student_hidden, "vocab", axis=1, tiled=True),
        lax.all_gather(teacher_hidden, "vocab", axis=1, tiled=True),
    )
    full_s, full_t = (
        lax.all_gather(wide_s, "dp", axis=0, tiled=True),
        lax.all_gather(wide_t, "dp", axis=0, tiled=True),
    )
    contract = (((1,), (1,)), ((), ()))
    teacher_logits = lax.dot_general(
        teacher_head, full_t, contract, preferred_element_type=jnp.float32
    )
    student_logits = lax.dot_general(
        student_head, full_s, contract, preferred_element_type=jnp.float32
    )
    local_t = jnp.max(teacher_logits, axis=0)
    local_s = jnp.max(student_logits, axis=0)
    teacher_max, student_max = lax.pmax((local_t, local_s), ("dp", "vocab"))
    teacher_exp = jnp.exp(teacher_logits - teacher_max)
    parts_t = jnp.sum(teacher_exp, axis=0)
    parts_s = jnp.sum(jnp.exp(student_logits - student_max), axis=0)
    parts_c = jnp.sum(teacher_exp * (teacher_logits - student_logits), axis=0)
    teacher_total, student_total, cross = lax.psum((parts_t, parts_s, parts_c), ("dp", "vocab"))
    teacher_lse = teacher_max + jnp.log(teacher_total)
    student_lse = student_max + jnp.log(student_total)
    kl = cross / teacher_total - teacher_lse + student_lse
    loss = jnp.mean(kl)
    logit_grad = (
        jnp.exp(student_logits - student_lse) - jnp.exp(teacher_logits - teacher_lse)
    ).astype(jnp.bfloat16)
    head_grad = jnp.dot(logit_grad, full_s, preferred_element_type=jnp.float32).astype(jnp.bfloat16)
    terms = lax.dot_general(
        logit_grad, student_head, (((0,), (0,)), ((), ())), preferred_element_type=jnp.float32
    )
    n_dp = lax.axis_size("dp")
    n_vocab = lax.axis_size("vocab")
    tok_rows = terms.shape[0] // n_dp
    feat_cols = terms.shape[1] // n_vocab
    ordered = (
        terms.reshape(n_dp, tok_rows, n_vocab, feat_cols)
        .transpose(0, 2, 1, 3)
        .reshape(n_dp * n_vocab * tok_rows, feat_cols)
    )
    hidden_grad = lax.psum_scatter(ordered, ("dp", "vocab"), scatter_dimension=0, tiled=True)
    return (loss, hidden_grad, head_grad)


def solution(mesh):
    placed = (
        P("dp", "vocab"),
        P("dp", "vocab"),
        P(("dp", "vocab"), None),
        P(("dp", "vocab"), None),
    )
    return jax.shard_map(
        local,
        mesh=mesh,
        in_specs=placed,
        out_specs=(P(), P("dp", "vocab"), P(("dp", "vocab"), None)),
        check_vma=False,
    )
```

profile of v0, /device:TPU:1, one launch (start us, length us, event | category | flops | bytes accessed | tf_op | source)
XLA Modules:
  0.0 1835.5 jit_solution(793848713444640825)
XLA Ops:
  7.2 0.0 copy-start
  7.2 0.0 all-gather.8.cloned.1.call-start
  7.2 38.8 %all-gather.1 = bf16[32,64,30]{1,2,0:T(8,128)(2,1)S(1)} all-gather(bf16[1,64,30]{1,2,0:T(8,128)(2,1)} %bitcast.23), channel_id=1, replica_groups=mesh['dp'=16,'vocab'=32] {'vocab'}, dimensions={0}, use_global_device_ids=true | all-gather | bytes 126720 | tf_op jit(solution)/shard_map/all_gather | solution.py:9
  46.1 0.1 copy.10
  46.2 0.9 reshape.21
  47.0 0.0 all-gather.8.cloned.1.call-update
  47.1 0.0 all-gather.6.cloned.1.call-start
  47.1 41.0 %all_gather.12 = bf16[30,4096]{1,0:T(8,128)(2,1)} all-gather(bf16[30,128]{1,0:T(8,128)(2,1)} %param.5), channel_id=1, replica_groups=mesh['dp'=16,'vocab'=32] {'vocab'}, dimensions={1}, use_global_device_ids=true | all-gather | bytes 253440 | tf_op jit(solution)/shard_map/all_gather | solution.py:10
  88.2 0.0 all-gather.6.cloned.1.call-update
  88.2 16.4 all-gather.8.cloned.1.call-done
  104.6 2.8 reshape.23
  107.4 2.7 fusion.2
  110.1 49.8 %all-gather.6.cloned.1.call-done = bf16[16,30,4096]{2,1,0:T(8,128)(2,1)} async-done(((bf16[1,30,4096]{2,1,0:T(8,128)(2,1)}), bf16[16,30,4096]{2,1,0:T(8,128)(2,1)}) %all-gather.6.cloned.1.call-update) | async-done | bytes 3932176 | tf_op jit(solution)/shard_map/all_gather | solution.py:14
  159.9 5.1 reshape.19
  165.0 3.4 fusion.3
  168.4 97.1 %all-reduce.3 = (f32[480]{0:T(512)S(1)}, f32[480]{0:T(512)S(1)}) all-reduce(f32[480]{0:T(512)S(1)} %get-tuple-element.14, f32[480]{0:T(512)S(1)} %get-tuple-element.16), channel_id=1, replica_groups=mesh['dp'=16,'vocab'=32] {'dp','vocab'}, use_global_device_ids=true, to_apply=%region_7.0 | all-reduce | flops 960 | bytes 7680 | tf_op jit(solution)/shard_map/pmax | solution.py:25
  265.5 0.5 multiply_reduce_fusion
  265.9 93.8 %all-reduce.2 = (f32[480]{0:T(512)S(1)}, f32[480]{0:T(512)S(1)}, f32[480]{0:T(512)S(1)}) all-reduce(f32[480]{0:T(512)S(1)} %get-tuple-element.5, f32[480]{0:T(512)S(1)} %get-tuple-element.4, f32[480]{0:T(512)S(1)} %get-tuple-element.3), channel_id=1, replica_groups=mesh['dp'=16,'vocab'=32] {'dp','vocab'}, use_global_device_ids=true, to_apply=%region_9.0 | all-reduce | flops 1440 | bytes 11520 | tf_op jit(solution)/shard_map/psum | solution.py:30
  359.7 0.6 add_reduce_fusion
  360.3 0.2 subtract_convert_fusion
  360.5 3.8 fusion.4
  364.3 7.5 reshape.16
  371.8 12.5 copy.13
  384.3 9.0 reshape.17
  393.3 1230.6 %fusion = f32[32,64]{1,0:T(8,128)S(1)} fusion(f32[15360,64]{1,0:T(8,128)} %reshape.17), kind=kCustom, calls=%all-reduce-scatter | all-reduce-scatter fusion | flops 1048577 | bytes 3940352
  1623.9 1.9 collective-permute-start.30
  1625.8 1.9 collective-permute-start.31
  1627.7 1.9 collective-permute-start.29
  1629.7 1.9 collective-permute-start.28
  1631.6 1.9 collective-permute-start.27
  1633.5 57.5 %collective-permute-done.31 = f32[30,64]{1,0:T(8,128)S(1)} collective-permute-done((f32[30,64]{1,0:T(8,128)S(1)}, f32[30,64]{1,0:T(8,128)S(1)}, u32[]{:S(2)}, u32[]{:S(2)}) %collective-permute-start.31) | collective-permute-done | bytes 7712
  1691.0 1.9 collective-permute-start.26
  1692.9 1.9 collective-permute-start.25
  1694.9 0.0 collective-permute-done.29
  1694.9 13.5 collective-permute-start.24
  1708.4 0.0 collective-permute-done.28
  1708.4 10.4 collective-permute-start.23
  1718.9 3.7 collective-permute-start.22
  1722.6 1.9 collective-permute-start.21
  1724.6 5.1 collective-permute-start.20
  1729.7 4.0 collective-permute-start.19
  1733.7 4.6 collective-permute-start.18
  1738.3 5.5 collective-permute-start.17
  1743.8 2.5 collective-permute-start.16
  1746.3 2.5 collective-permute-start.15
  1748.9 5.2 collective-permute-start.14
  1754.1 3.7 collective-permute-start.13
  1757.8 2.8 collective-permute-start.12
  1760.7 3.2 collective-permute-start.11
  1763.8 7.3 collective-permute-start.10
  1771.1 2.3 collective-permute-start.9
  1773.5 14.7 collective-permute-start.8
  1788.1 3.1 collective-permute-start.7
  1791.2 8.2 collective-permute-start.6
  1799.5 1.9 collective-permute-start.5
  1801.4 2.4 collective-permute-start.4
  1803.8 2.4 collective-permute-start.3
  1806.2 5.2 collective-permute-start.2
  1811.3 3.1 collective-permute-start.1
  1814.4 1.9 collective-permute-start
  1816.4 3.2 convolution_convert_fusion
  1820.3 2.5 collective-permute-done
  1822.8 4.0 concatenate
  1826.9 0.6 constant_dynamic-slice_fusion
  (30 shorter events, 0.1 us)
Async XLA Ops:
  7.2 157.8 %copy-start = (bf16[250,4096]{1,0:T(8,128)(2,1)S(1)}, bf16[250,4096]{1,0:T(8,128)(2,1)}, u32[]{:S(2)}) copy-start(bf16[250,4096]{1,0:T(8,128)(2,1)} %param.7) | copy-start | bytes 6144004
  7.2 97.5 %all-gather.8.cloned.1.call-start = ((), (), s32[]{:S(2)}) async-start(), calls=%async_computation.1 | async-start | bytes 2228224 | tf_op jit(solution)/shard_map/all_gather | solution.py:13
  47.1 112.8 %all-gather.6.cloned.1.call-start = ((), (), s32[]{:S(2)}) async-start(), calls=%async_computation | async-start | bytes 4456448 | tf_op jit(solution)/shard_map/all_gather | solution.py:14
  1623.9 69.1 %collective-permute-start.30 = (f32[32,64]{1,0:T(8,128)S(1)}, f32[32,64]{1,0:T(8,128)S(1)}, u32[]{:S(2)}, u32[]{:S(2)}) collective-permute-start(f32[32,64]{1,0:T(8,128)S(1)} %fusion), channel_id=1, source_target_pairs={{0,31},{1,32},{2,33},{3,34},{4,35},{5,36},{6,37},{7,38},{8,39},{9,... | collective-permute-start | bytes 24584
  1625.8 65.2 %collective-permute-start.31 = (f32[30,64]{1,0:T(8,128)S(1)}, f32[30,64]{1,0:T(8,128)S(1)}, u32[]{:S(2)}, u32[]{:S(2)}) collective-permute-start(f32[30,64]{1,0:T(8,128)S(1)} %slice), channel_id=1, source_target_pairs={{0,32},{1,33},{2,34},{3,35},{4,36},{5,37},{6,38},{7,39},{8,40},{9,... | collective-permute-start | bytes 23048
  1627.7 67.1 %collective-permute-start.29 = (f32[32,64]{1,0:T(8,128)S(1)}, f32[32,64]{1,0:T(8,128)S(1)}, u32[]{:S(2)}, u32[]{:S(2)}) collective-permute-start(f32[32,64]{1,0:T(8,128)S(1)} %fusion), channel_id=1, source_target_pairs={{0,30},{1,31},{2,32},{3,33},{4,34},{5,35},{6,36},{7,37},{8,38},{9,... | collective-permute-start | bytes 24584
  1629.7 78.7 %collective-permute-start.28 = (f32[32,64]{1,0:T(8,128)S(1)}, f32[32,64]{1,0:T(8,128)S(1)}, u32[]{:S(2)}, u32[]{:S(2)}) collective-permute-start(f32[32,64]{1,0:T(8,128)S(1)} %fusion), channel_id=1, source_target_pairs={{0,29},{1,30},{2,31},{3,32},{4,33},{5,34},{6,35},{7,36},{8,37},{9,... | collective-permute-start | bytes 24584
  1631.6 87.3 %collective-permute-start.27 = (f32[32,64]{1,0:T(8,128)S(1)}, f32[32,64]{1,0:T(8,128)S(1)}, u32[]{:S(2)}, u32[]{:S(2)}) collective-permute-start(f32[32,64]{1,0:T(8,128)S(1)} %fusion), channel_id=1, source_target_pairs={{0,28},{1,29},{2,30},{3,31},{4,32},{5,33},{6,34},{7,35},{8,36},{9,... | collective-permute-start | bytes 24584
  1691.0 31.6 %collective-permute-start.26 = (f32[32,64]{1,0:T(8,128)S(1)}, f32[32,64]{1,0:T(8,128)S(1)}, u32[]{:S(2)}, u32[]{:S(2)}) collective-permute-start(f32[32,64]{1,0:T(8,128)S(1)} %fusion), channel_id=1, source_target_pairs={{0,27},{1,28},{2,29},{3,30},{4,31},{5,32},{6,33},{7,34},{8,35},{9,... | collective-permute-start | bytes 24584
  1692.9 31.6 %collective-permute-start.25 = (f32[32,64]{1,0:T(8,128)S(1)}, f32[32,64]{1,0:T(8,128)S(1)}, u32[]{:S(2)}, u32[]{:S(2)}) collective-permute-start(f32[32,64]{1,0:T(8,128)S(1)} %fusion), channel_id=1, source_target_pairs={{0,26},{1,27},{2,28},{3,29},{4,30},{5,31},{6,32},{7,33},{8,34},{9,... | collective-permute-start | bytes 24584
  1694.9 34.8 %collective-permute-start.24 = (f32[32,64]{1,0:T(8,128)S(1)}, f32[32,64]{1,0:T(8,128)S(1)}, u32[]{:S(2)}, u32[]{:S(2)}) collective-permute-start(f32[32,64]{1,0:T(8,128)S(1)} %fusion), channel_id=1, source_target_pairs={{0,25},{1,26},{2,27},{3,28},{4,29},{5,30},{6,31},{7,32},{8,33},{9,... | collective-permute-start | bytes 24584
  1708.4 25.2 %collective-permute-start.23 = (f32[32,64]{1,0:T(8,128)S(1)}, f32[32,64]{1,0:T(8,128)S(1)}, u32[]{:S(2)}, u32[]{:S(2)}) collective-permute-start(f32[32,64]{1,0:T(8,128)S(1)} %fusion), channel_id=1, source_target_pairs={{0,24},{1,25},{2,26},{3,27},{4,28},{5,29},{6,30},{7,31},{8,32},{9,... | collective-permute-start | bytes 24584
  1718.9 19.4 %collective-permute-start.22 = (f32[32,64]{1,0:T(8,128)S(1)}, f32[32,64]{1,0:T(8,128)S(1)}, u32[]{:S(2)}, u32[]{:S(2)}) collective-permute-start(f32[32,64]{1,0:T(8,128)S(1)} %fusion), channel_id=1, source_target_pairs={{0,23},{1,24},{2,25},{3,26},{4,27},{5,28},{6,29},{7,30},{8,31},{9,... | collective-permute-start | bytes 24584
  1722.6 21.2 %collective-permute-start.21 = (f32[32,64]{1,0:T(8,128)S(1)}, f32[32,64]{1,0:T(8,128)S(1)}, u32[]{:S(2)}, u32[]{:S(2)}) collective-permute-start(f32[32,64]{1,0:T(8,128)S(1)} %fusion), channel_id=1, source_target_pairs={{0,22},{1,23},{2,24},{3,25},{4,26},{5,27},{6,28},{7,29},{8,30},{9,... | collective-permute-start | bytes 24584
  1724.6 21.8 %collective-permute-start.20 = (f32[32,64]{1,0:T(8,128)S(1)}, f32[32,64]{1,0:T(8,128)S(1)}, u32[]{:S(2)}, u32[]{:S(2)}) collective-permute-start(f32[32,64]{1,0:T(8,128)S(1)} %fusion), channel_id=1, source_target_pairs={{0,21},{1,22},{2,23},{3,24},{4,25},{5,26},{6,27},{7,28},{8,29},{9,... | collective-permute-start | bytes 24584
  1729.7 19.2 %collective-permute-start.19 = (f32[32,64]{1,0:T(8,128)S(1)}, f32[32,64]{1,0:T(8,128)S(1)}, u32[]{:S(2)}, u32[]{:S(2)}) collective-permute-start(f32[32,64]{1,0:T(8,128)S(1)} %fusion), channel_id=1, source_target_pairs={{0,20},{1,21},{2,22},{3,23},{4,24},{5,25},{6,26},{7,27},{8,28},{9,... | collective-permute-start | bytes 24584
  1733.7 20.4 %collective-permute-start.18 = (f32[32,64]{1,0:T(8,128)S(1)}, f32[32,64]{1,0:T(8,128)S(1)}, u32[]{:S(2)}, u32[]{:S(2)}) collective-permute-start(f32[32,64]{1,0:T(8,128)S(1)} %fusion), channel_id=1, source_target_pairs={{0,19},{1,20},{2,21},{3,22},{4,23},{5,24},{6,25},{7,26},{8,27},{9,... | collective-permute-start | bytes 24584
  1738.3 19.5 %collective-permute-start.17 = (f32[32,64]{1,0:T(8,128)S(1)}, f32[32,64]{1,0:T(8,128)S(1)}, u32[]{:S(2)}, u32[]{:S(2)}) collective-permute-start(f32[32,64]{1,0:T(8,128)S(1)} %fusion), channel_id=1, source_target_pairs={{0,18},{1,19},{2,20},{3,21},{4,22},{5,23},{6,24},{7,25},{8,26},{9,... | collective-permute-start | bytes 24584
  1743.8 16.8 collective-permute-start.16
  1746.3 17.5 collective-permute-start.15
  1748.9 22.2 %collective-permute-start.14 = (f32[32,64]{1,0:T(8,128)S(1)}, f32[32,64]{1,0:T(8,128)S(1)}, u32[]{:S(2)}, u32[]{:S(2)}) collective-permute-start(f32[32,64]{1,0:T(8,128)S(1)} %fusion), channel_id=1, source_target_pairs={{0,15},{1,16},{2,17},{3,18},{4,19},{5,20},{6,21},{7,22},{8,23},{9,... | collective-permute-start | bytes 24584
  1754.1 19.3 %collective-permute-start.13 = (f32[32,64]{1,0:T(8,128)S(1)}, f32[32,64]{1,0:T(8,128)S(1)}, u32[]{:S(2)}, u32[]{:S(2)}) collective-permute-start(f32[32,64]{1,0:T(8,128)S(1)} %fusion), channel_id=1, source_target_pairs={{0,14},{1,15},{2,16},{3,17},{4,18},{5,19},{6,20},{7,21},{8,22},{9,... | collective-permute-start | bytes 24584
  1757.8 30.3 %collective-permute-start.12 = (f32[32,64]{1,0:T(8,128)S(1)}, f32[32,64]{1,0:T(8,128)S(1)}, u32[]{:S(2)}, u32[]{:S(2)}) collective-permute-start(f32[32,64]{1,0:T(8,128)S(1)} %fusion), channel_id=1, source_target_pairs={{0,13},{1,14},{2,15},{3,16},{4,17},{5,18},{6,19},{7,20},{8,21},{9,... | collective-permute-start | bytes 24584
  1760.7 30.5 %collective-permute-start.11 = (f32[32,64]{1,0:T(8,128)S(1)}, f32[32,64]{1,0:T(8,128)S(1)}, u32[]{:S(2)}, u32[]{:S(2)}) collective-permute-start(f32[32,64]{1,0:T(8,128)S(1)} %fusion), channel_id=1, source_target_pairs={{0,12},{1,13},{2,14},{3,15},{4,16},{5,17},{6,18},{7,19},{8,20},{9,... | collective-permute-start | bytes 24584
  1763.8 35.6 %collective-permute-start.10 = (f32[32,64]{1,0:T(8,128)S(1)}, f32[32,64]{1,0:T(8,128)S(1)}, u32[]{:S(2)}, u32[]{:S(2)}) collective-permute-start(f32[32,64]{1,0:T(8,128)S(1)} %fusion), channel_id=1, source_target_pairs={{0,11},{1,12},{2,13},{3,14},{4,15},{5,16},{6,17},{7,18},{8,19},{9,... | collective-permute-start | bytes 24584
  1771.1 30.3 %collective-permute-start.9 = (f32[32,64]{1,0:T(8,128)S(1)}, f32[32,64]{1,0:T(8,128)S(1)}, u32[]{:S(2)}, u32[]{:S(2)}) collective-permute-start(f32[32,64]{1,0:T(8,128)S(1)} %fusion), channel_id=1, source_target_pairs={{0,10},{1,11},{2,12},{3,13},{4,14},{5,15},{6,16},{7,17},{8,18},{9,... | collective-permute-start | bytes 24584
  1773.5 30.3 %collective-permute-start.8 = (f32[32,64]{1,0:T(8,128)S(1)}, f32[32,64]{1,0:T(8,128)S(1)}, u32[]{:S(2)}, u32[]{:S(2)}) collective-permute-start(f32[32,64]{1,0:T(8,128)S(1)} %fusion), channel_id=1, source_target_pairs={{0,9},{1,10},{2,11},{3,12},{4,13},{5,14},{6,15},{7,16},{8,17},{9,1... | collective-permute-start | bytes 24584
  1788.1 18.0 collective-permute-start.7
  1791.2 20.1 %collective-permute-start.6 = (f32[32,64]{1,0:T(8,128)S(1)}, f32[32,64]{1,0:T(8,128)S(1)}, u32[]{:S(2)}, u32[]{:S(2)}) collective-permute-start(f32[32,64]{1,0:T(8,128)S(1)} %fusion), channel_id=1, source_target_pairs={{0,7},{1,8},{2,9},{3,10},{4,11},{5,12},{6,13},{7,14},{8,15},{9,16}... | collective-permute-start | bytes 24584
  1799.5 15.0 collective-permute-start.5
  1801.4 18.9 %collective-permute-start.4 = (f32[32,64]{1,0:T(8,128)S(1)}, f32[32,64]{1,0:T(8,128)S(1)}, u32[]{:S(2)}, u32[]{:S(2)}) collective-permute-start(f32[32,64]{1,0:T(8,128)S(1)} %fusion), channel_id=1, source_target_pairs={{0,5},{1,6},{2,7},{3,8},{4,9},{5,10},{6,11},{7,12},{8,13},{9,14},{... | collective-permute-start | bytes 24584
  1803.8 16.5 collective-permute-start.3
  1806.2 14.1 collective-permute-start.2
  1811.3 9.0 collective-permute-start.1
  1814.4 8.4 collective-permute-start
Sparse Core Ops, SparseCore 0:
  47.2 57.3 all-gather.7
  106.7 53.1 all-gather.5
where the time goes:
time: 1840 us
  blocking collectives  1500 us (82%)
  starting transfers between devices  135 us (7%)
  waiting for transfers between devices  126 us (7%)
  local copies, waits for them, and re-layouts  42.4 us (2%)
    unnamed x1, blocking collectives  1230 us
    unnamed x32, starting transfers between devices  134 us
    pmax x1, blocking collectives, local(): teacher_max, student_max = lax.pmax((local_t, local_s), ('dp', 'vocab'))  97.1 us
    psum x1, blocking collectives, local(): lax.psum((parts_t, parts_s, parts_c), ('dp', 'vocab'))  93.8 us
    unnamed x34, waiting for transfers between devices  60.1 us
    all_gather x1, waiting for transfers between devices, local(): lax.all_gather(wide_t, 'dp', axis=0, tiled=True)  49.8 us
    all_gather x1, blocking collectives, local(): lax.all_gather(teacher_hidden, 'vocab', axis=1, tiled=True)  41 us
    all_gather x1, blocking collectives, local(): lax.all_gather(student_hidden, 'vocab', axis=1, tiled=True)  38.8 us
  transfers between devices with their start and end apart: 34, of which 4 were waited for; matrix products, arithmetic and copies ran while one was open for 0% of the time, Pallas kernels for 0%

commit v1 on v0

v1 whole, which is shorter than its diff:
```python
import jax
import jax.numpy as jnp
from jax import lax
from jax.sharding import Mesh, PartitionSpec as P

BF = jnp.bfloat16
F32 = jnp.float32
Z, Y, X = 8, 8, 4
TOK = 30
PAD = 32


def exchange(v, axes):
    return lax.all_to_all(v, axes, 0, 0, tiled=True)


def spread(v, axes, n):
    return exchange(jnp.broadcast_to(v[None], (n,) + v.shape), axes)


def swap(v):
    return lax.ppermute(v, "core", [(0, 1), (1, 0)])


def merge(parts):
    m = jnp.max(parts[:, 0:2], axis=0)
    w = jnp.exp(parts[:, 0:2] - m)
    total = jnp.sum(w * parts[:, 2:4], axis=0)
    cross = jnp.sum(w[:, 0:1] * parts[:, 4:5], axis=0)
    return jnp.concatenate([m, total, cross, jnp.zeros((3, m.shape[1]), F32)], axis=0)


def local(student_hidden, teacher_hidden, student_head, teacher_head):
    other_s = swap(student_head)
    other_t = swap(teacher_head)
    fs, ft = student_hidden.shape[1], teacher_hidden.shape[1]
    half = PAD // 2

    sp = jnp.pad(student_hidden, ((0, PAD - TOK), (0, 0)))
    tp = jnp.pad(teacher_hidden, ((0, PAD - TOK), (0, 0)))
    message = jnp.concatenate([tp, jnp.concatenate([sp[:half], sp[half:]], axis=1)], axis=0)
    near = spread(message, ("z", "y"), Z * Y).reshape(Z, Y, PAD + half, ft)
    near_t = near[:, :, :PAD].transpose(0, 2, 1, 3).reshape(Z * PAD, Y * ft)
    near_s = near[:, :, PAD:].reshape(Z, Y, half, 2, fs).transpose(0, 3, 2, 1, 4).reshape(Z * PAD, Y * fs)
    wide = spread(jnp.concatenate([near_t, near_s], axis=1), "x", X)
    full_t = wide[:, :, : Y * ft].reshape(X, Z * PAD, Y, ft).transpose(1, 2, 0, 3).reshape(Z * PAD, X * Y * ft)
    full_s = wide[:, :, Y * ft :].reshape(X, Z * PAD, Y, fs).transpose(1, 2, 0, 3).reshape(Z * PAD, X * Y * fs)

    nt = (((1,), (1,)), ((), ()))
    heads = ((student_head, teacher_head), (other_s, other_t))
    logits = [
        (
            lax.dot_general(hs, full_s, nt, preferred_element_type=F32),
            lax.dot_general(ht, full_t, nt, preferred_element_type=F32),
        )
        for hs, ht in heads
    ]
    stats = []
    for ls, lt in logits:
        mt = jnp.max(lt, axis=0)
        ms = jnp.max(ls, axis=0)
        et = jnp.exp(lt - mt)
        zero = jnp.zeros_like(mt)
        stats.append(
            jnp.stack(
                [
                    mt,
                    ms,
                    jnp.sum(et, axis=0),
                    jnp.sum(jnp.exp(ls - ms), axis=0),
                    jnp.sum(et * (lt - ls), axis=0),
                    zero,
                    zero,
                    zero,
                ]
            )
        )
    mine = merge(jnp.stack(stats))
    plane = merge(spread(mine, ("y", "x"), Y * X))
    whole = merge(spread(plane, "z", Z))
    lse_t = whole[0] + jnp.log(whole[2])
    lse_s = whole[1] + jnp.log(whole[3])
    kl = whole[4] / whole[2] - lse_t + lse_s
    real = (lax.iota(jnp.int32, Z * PAD) % PAD) < TOK
    part = jnp.sum(jnp.where(real, kl, 0.0))
    loss = (part + swap(part[None])[0]) / (2 * Z * TOK)

    grads = [(jnp.exp(ls - lse_s) - jnp.exp(lt - lse_t)).astype(BF) for ls, lt in logits]
    sent = jnp.dot(grads[1], full_s, preferred_element_type=F32).astype(BF)
    arrived = swap(sent)
    tn = (((0,), (0,)), ((), ()))
    terms = lax.dot_general(grads[0], student_head, tn, preferred_element_type=F32) + lax.dot_general(
        grads[1], other_s, tn, preferred_element_type=F32
    )
    by_x = terms.reshape(Z * PAD, Y, X, fs).transpose(2, 0, 1, 3).reshape(X, Z * PAD, Y * fs).astype(BF)
    row = jnp.sum(exchange(by_x, "x").astype(F32), axis=0)
    by_zy = (
        row.reshape(Z, 2, half, Y, fs).transpose(0, 3, 2, 1, 4).reshape(Z * Y, half, 2 * fs).astype(BF)
    )
    mine_h = jnp.sum(exchange(by_zy, ("z", "y")).astype(F32), axis=0)
    hidden_grad = jnp.concatenate([mine_h[:, :fs], mine_h[:, fs:]], axis=0)[:TOK]
    kept = jnp.dot(grads[0], full_s, preferred_element_type=F32)
    head_grad = (kept + arrived.astype(F32)).astype(BF)
    return (loss, hidden_grad, head_grad)


def solution(mesh):
    fine = Mesh(mesh.devices.reshape(Z, 2, Y, X), ("z", "core", "y", "x"))
    rows, cols = ("z", "core"), ("y", "x")
    return jax.shard_map(
        local,
        mesh=fine,
        in_specs=(P(rows, cols), P(rows, cols), P(rows + cols, None), P(rows + cols, None)),
        out_specs=(P(), P(rows, cols), P(rows + cols, None)),
        check_vma=False,
    )
```

time: 1840 us -> 175 us (0.10)
  the two profiles are of different devices: /device:TPU:1 before, /device:TPU:8 now
where the time goes in v1:
time: 175 us; the launch traced here: 174 us
  blocking collectives  87.5 us (50%)
  waiting for transfers between devices  38.5 us (22%)
  starting transfers between devices  17.6 us (10%)
  local copies, waits for them, and re-layouts  12.5 us (7%)
  matrix products  11.6 us (7%)
  between operations  3.37 us (2%)
  other arithmetic  3.29 us (2%)
    all_to_all x4, blocking collectives, exchange(): return lax.all_to_all(v, axes, 0, 0, tiled=True)  87.5 us
    all_to_all x2, waiting for transfers between devices, exchange(): return lax.all_to_all(v, axes, 0, 0, tiled=True)  37.3 us
    all_to_all x2, starting transfers between devices, exchange(): return lax.all_to_all(v, axes, 0, 0, tiled=True)  9.42 us
    ppermute x4, starting transfers between devices, swap(): return lax.ppermute(v, 'core', [(0, 1), (1, 0)])  8.14 us
    unnamed x11, local copies, waits for them, and re-layouts  3.72 us
  transfers between devices with their start and end apart: 6, of which 3 were waited for; matrix products, arithmetic and copies ran while one was open for 7% of the time, Pallas kernels for 0%

profile of v1, /device:TPU:8, one launch (start us, length us, event | category | flops | bytes accessed | tf_op | source)
XLA Modules:
  0.0 174.3 jit_solution(18424833567384100273)
XLA Ops:
  0.6 0.7 fusion.16
  1.3 0.8 fusion.7
  2.1 0.1 broadcast_in_dim.13
  2.2 40.4 %all_to_all.30 = bf16[64,48,128]{2,1,0:T(8,128)(2,1)S(1)} all-to-all(bf16[64,48,128]{2,1,0:T(8,128)(2,1)S(1)} %broadcast_in_dim.13), channel_id=1, replica_groups=mesh['z'=8,'core'=2,'y'=8,'x'=4] {'z','y'}, dimensions={0} | all-to-all | bytes 1572864 | tf_op jit(solution)/shard_map/all_to_all | solution.py:14
  42.6 0.2 copy.40
  42.9 0.1 copy.70
  43.0 0.2 reshape.57
  43.2 0.2 copy.41
  43.4 0.3 reshape.58
  43.8 0.1 pad_maximum_fusion
  43.8 0.3 copy.42
  44.1 1.9 %broadcast_in_dim.14 = bf16[4,256,1536]{1,2,0:T(8,128)(2,1)} broadcast(bf16[256,1536]{0,1:T(8,128)(2,1)S(1)} %copy.42), dimensions={1,2} | broadcast | bytes 3932160 | tf_op jit(solution)/shard_map/broadcast_in_dim | solution.py:18
  46.0 4.3 %all-to-all-start.1 = ((bf16[4,256,1536]{1,2,0:T(8,128)(2,1)}), bf16[4,256,1536]{1,2,0:T(8,128)(2,1)S(1)}, u32[]{:S(2)}, u32[]{:S(2)}) async-start(bf16[4,256,1536]{1,2,0:T(8,128)(2,1)} %broadcast_in_dim.14), calls=%async_computation.1 | async-start | bytes 6291456 | tf_op jit(solution)/shard_map/all_to_all | solution.py:14
  50.3 1.9 %collective-permute-start = (bf16[250,4096]{1,0:T(8,128)(2,1)}, bf16[250,4096]{1,0:T(8,128)(2,1)}, u32[]{:S(2)}, u32[]{:S(2)}) collective-permute-start(bf16[250,4096]{1,0:T(8,128)(2,1)} %param.7), channel_id=1, source_target_pairs={{0,32},{32,0},{1,33},{33,1},{2,34},{34,2},{3,35},{35,3},{4,36},{36... | collective-permute-start | bytes 6144008 | tf_op jit(solution)/shard_map/ppermute | solution.py:22
  52.2 2.4 %collective-permute-start.1 = (bf16[250,2048]{1,0:T(8,128)(2,1)}, bf16[250,2048]{1,0:T(8,128)(2,1)}, u32[]{:S(2)}, u32[]{:S(2)}) collective-permute-start(bf16[250,2048]{1,0:T(8,128)(2,1)} %param.6), channel_id=1, source_target_pairs={{0,32},{32,0},{1,33},{33,1},{2,34},{34,2},{3,35},{35,3},{4,36},{36... | collective-permute-start | bytes 3072008 | tf_op jit(solution)/shard_map/ppermute | solution.py:22
  54.6 0.1 pad.19.clone
  54.7 30.8 %all-to-all-done.1 = bf16[4,256,1536]{1,2,0:T(8,128)(2,1)S(1)} async-done(((bf16[4,256,1536]{1,2,0:T(8,128)(2,1)}), bf16[4,256,1536]{1,2,0:T(8,128)(2,1)S(1)}, u32[]{:S(2)}, u32[]{:S(2)}) %all-to-all-start.1) | async-done | bytes 3145760 | tf_op jit(solution)/shard_map/all_to_all | solution.py:14
  85.5 0.1 slice.108
  85.6 1.6 copy-done
  87.2 0.1 copy.44
  87.3 0.0 slice-start
  87.3 1.6 slice-done
  88.9 0.2 copy.43
  89.1 0.0 copy-start.4
  89.1 1.2 copy-done.1
  90.3 0.5 fusion.20
  90.8 0.8 copy-done.4
  91.6 0.7 fusion.19
  92.3 0.1 multiply_reduce_fusion.1
  92.5 0.0 collective-permute-done.1
  92.5 1.8 %fusion.18 = (f32[256]{0:T(256)S(1)}, f32[256,250]{0,1:T(8,128)S(1)}) fusion(bf16[256,2048]{0,1:T(8,128)(2,1)S(1)} %bitcast.62, bf16[250,2048]{1,0:T(8,128)(2,1)} %collective-permute-done.1), kind=kOutput, calls=%fused_computation.54 | convolution fusion | flops 262207744 | bytes 2329600 | tf_op jit(solution)/shard_map/dot_general | solution.py:53
  94.4 0.0 collective-permute-done
  94.4 0.0 copy-done.3
  94.4 2.3 %fusion.17 = (f32[256]{0:T(256)S(1)}, f32[256,250]{0,1:T(8,128)S(1)}) fusion(bf16[256,4096]{0,1:T(8,128)(2,1)S(1)} %bitcast.73, bf16[250,4096]{1,0:T(8,128)(2,1)} %collective-permute-done), kind=kOutput, calls=%fused_computation.53 | convolution fusion | flops 524351744 | bytes 4402176 | tf_op jit(solution)/shard_map/dot_general | solution.py:54
  96.7 0.1 multiply_reduce_fusion
  97.0 0.1 maximum_maximum_fusion
  97.1 17.1 %all_to_all.31 = f32[32,8,256]{2,1,0:T(8,128)S(1)} all-to-all(f32[32,8,256]{2,1,0:T(8,128)S(1)} %broadcast_in_dim.15), channel_id=1, replica_groups=mesh['z'=8,'core'=2,'y'=8,'x'=4] {'y','x'}, dimensions={0} | all-to-all | bytes 524288 | tf_op jit(solution)/shard_map/all_to_all | solution.py:14
  114.2 0.1 fusion.3
  114.3 0.1 fusion.4
  114.4 0.1 maximum_maximum_fusion.1
  114.5 11.5 %all_to_all.32 = f32[8,8,256]{2,1,0:T(8,128)S(1)} all-to-all(f32[8,8,256]{2,1,0:T(8,128)S(1)} %broadcast_in_dim.16), channel_id=1, replica_groups=mesh['z'=8,'core'=2,'y'=8,'x'=4] {'z'}, dimensions={0} | all-to-all | bytes 131072 | tf_op jit(solution)/shard_map/all_to_all | solution.py:14
  126.1 0.2 subtract_convert_fusion
  126.2 1.4 convolution_convert_fusion
  127.7 1.9 %collective-permute-start.3 = (bf16[250,2048]{1,0:T(8,128)(2,1)}, bf16[250,2048]{1,0:T(8,128)(2,1)}, u32[]{:S(2)}, u32[]{:S(2)}) collective-permute-start(bf16[250,2048]{1,0:T(8,128)(2,1)} %convolution_convert_fusion), channel_id=1, source_target_pairs={{0,32},{32,0},{1,33},{33,1},{2,34},{34,2},{3,35},{35,3},{4,36},{36... | collective-permute-start | bytes 3072008 | tf_op jit(solution)/shard_map/ppermute | solution.py:22
  129.6 0.5 fusion.21
  130.1 1.7 fusion
  131.8 0.5 copy.54
  132.3 0.1 copy.55
  132.4 18.5 %all_to_all.33 = bf16[4,256,512]{1,2,0:T(8,128)(2,1)S(1)} all-to-all(bf16[4,256,512]{1,2,0:T(8,128)(2,1)S(1)} %bitcast.67), channel_id=1, replica_groups=mesh['z'=8,'core'=2,'y'=8,'x'=4] {'x'}, dimensions={0} | all-to-all | bytes 2097152 | tf_op jit(solution)/shard_map/all_to_all | solution.py:14
  150.9 0.3 reduce_sum.157
  151.1 0.1 copy.56
  151.3 0.3 convert_element_type.53
  151.6 0.5 copy.57
  152.1 1.0 convert_element_type.55
  153.1 5.1 %all-to-all-start.5 = ((bf16[64,16,128]{2,1,0:T(8,128)(2,1)}), bf16[64,16,128]{2,1,0:T(8,128)(2,1)S(1)}, u32[]{:S(2)}, u32[]{:S(2)}) async-start(bf16[64,16,128]{2,1,0:T(8,128)(2,1)} %convert_element_type.55), calls=%async_computation.5 | async-start | bytes 524288 | tf_op jit(solution)/shard_map/all_to_all | solution.py:14
  158.2 0.6 fusion.13
  158.9 1.9 %collective-permute-start.2 = (f32[1]{0:T(128)}, f32[1]{0:T(128)}, u32[]{:S(2)}, u32[]{:S(2)}) collective-permute-start(f32[1]{0:T(128)} %bitcast.25), channel_id=1, source_target_pairs={{0,32},{32,0},{1,33},{33,1},{2,34},{34,2},{3,35},{35,3},{4,36},{36... | collective-permute-start | bytes 20 | tf_op jit(solution)/shard_map/ppermute | solution.py:22
  160.8 1.2 collective-permute-done.2
  163.3 0.0 collective-permute-done.3
  163.3 2.7 %add_convert_fusion = bf16[250,2048]{1,0:T(8,128)(2,1)} fusion(bf16[250,2048]{1,0:T(8,128)(2,1)} %collective-permute-done.3, bf16[256,250]{0,1:T(8,128)(2,1)S(1)} %get-tuple-element.22, bf16[256,2048]{0,1:T(8,128)(2,1)S(1)} %bitcast.64), kind=kOutput, calls=%fused_computation.3 | convolution fusion | flops 263680000 | bytes 3224576 | tf_op jit(solution)/shard_map/dot_general | solution.py:102
  165.9 6.4 %all-to-all-done.5 = bf16[64,16,128]{2,1,0:T(8,128)(2,1)S(1)} async-done(((bf16[64,16,128]{2,1,0:T(8,128)(2,1)}), bf16[64,16,128]{2,1,0:T(8,128)(2,1)S(1)}, u32[]{:S(2)}, u32[]{:S(2)}) %all-to-all-start.5) | async-done | bytes 262176 | tf_op jit(solution)/shard_map/all_to_all | solution.py:14
  172.4 0.1 convert_reduce_fusion
  172.4 0.1 fusion.15
  172.5 0.6 pad_maximum_fusion.1
  (24 shorter events, 0.4 us)
Async XLA Ops:
  46.0 39.6 %all-to-all-start.1 = ((bf16[4,256,1536]{1,2,0:T(8,128)(2,1)}), bf16[4,256,1536]{1,2,0:T(8,128)(2,1)S(1)}, u32[]{:S(2)}, u32[]{:S(2)}) async-start(bf16[4,256,1536]{1,2,0:T(8,128)(2,1)} %broadcast_in_dim.14), calls=%async_computation.1 | async-start | bytes 6291456 | tf_op jit(solution)/shard_map/all_to_all | solution.py:14
  50.3 44.1 %collective-permute-start = (bf16[250,4096]{1,0:T(8,128)(2,1)}, bf16[250,4096]{1,0:T(8,128)(2,1)}, u32[]{:S(2)}, u32[]{:S(2)}) collective-permute-start(bf16[250,4096]{1,0:T(8,128)(2,1)} %param.7), channel_id=1, source_target_pairs={{0,32},{32,0},{1,33},{33,1},{2,34},{34,2},{3,35},{35,3},{4,36},{36... | collective-permute-start | bytes 6144008 | tf_op jit(solution)/shard_map/ppermute | solution.py:22
  52.2 40.3 %collective-permute-start.1 = (bf16[250,2048]{1,0:T(8,128)(2,1)}, bf16[250,2048]{1,0:T(8,128)(2,1)}, u32[]{:S(2)}, u32[]{:S(2)}) collective-permute-start(bf16[250,2048]{1,0:T(8,128)(2,1)} %param.6), channel_id=1, source_target_pairs={{0,32},{32,0},{1,33},{33,1},{2,34},{34,2},{3,35},{35,3},{4,36},{36... | collective-permute-start | bytes 3072008 | tf_op jit(solution)/shard_map/ppermute | solution.py:22
  85.5 1.7 copy-start
  87.3 1.6 slice-start
  88.9 1.4 copy-start.1
  89.1 3.2 %copy-start.2 = (bf16[256,8,4,128]{0,3,2,1:T(8,128)(2,1)}, bf16[256,8,4,128]{0,3,2,1:T(8,128)(2,1)S(1)}, u32[]{:S(2)}) copy-start(bf16[256,8,4,128]{0,3,2,1:T(8,128)(2,1)S(1)} %copy.43) | copy-start | bytes 6291460
  89.1 2.5 %copy-start.4 = (bf16[250,4096]{1,0:T(8,128)(2,1)S(1)}, bf16[250,4096]{1,0:T(8,128)(2,1)}, u32[]{:S(2)}) copy-start(bf16[250,4096]{1,0:T(8,128)(2,1)} %param.7) | copy-start | bytes 6144004
  92.5 1.9 %copy-start.3 = (bf16[256,8,4,128]{0,3,2,1:T(8,128)(2,1)S(1)}, bf16[256,8,4,128]{0,3,2,1:T(8,128)(2,1)}, u32[]{:S(2)}) copy-start(bf16[256,8,4,128]{0,3,2,1:T(8,128)(2,1)} %copy-done.2) | copy-start | bytes 6291460
  127.7 35.6 %collective-permute-start.3 = (bf16[250,2048]{1,0:T(8,128)(2,1)}, bf16[250,2048]{1,0:T(8,128)(2,1)}, u32[]{:S(2)}, u32[]{:S(2)}) collective-permute-start(bf16[250,2048]{1,0:T(8,128)(2,1)} %convolution_convert_fusion), channel_id=1, source_target_pairs={{0,32},{32,0},{1,33},{33,1},{2,34},{34,2},{3,35},{35,3},{4,36},{36... | collective-permute-start | bytes 3072008 | tf_op jit(solution)/shard_map/ppermute | solution.py:22
  153.1 19.3 %all-to-all-start.5 = ((bf16[64,16,128]{2,1,0:T(8,128)(2,1)}), bf16[64,16,128]{2,1,0:T(8,128)(2,1)S(1)}, u32[]{:S(2)}, u32[]{:S(2)}) async-start(bf16[64,16,128]{2,1,0:T(8,128)(2,1)} %convert_element_type.55), calls=%async_computation.5 | async-start | bytes 524288 | tf_op jit(solution)/shard_map/all_to_all | solution.py:14
  158.9 3.1 %collective-permute-start.2 = (f32[1]{0:T(128)}, f32[1]{0:T(128)}, u32[]{:S(2)}, u32[]{:S(2)}) collective-permute-start(f32[1]{0:T(128)} %bitcast.25), channel_id=1, source_target_pairs={{0,32},{32,0},{1,33},{33,1},{2,34},{34,2},{3,35},{35,3},{4,36},{36... | collective-permute-start | bytes 20 | tf_op jit(solution)/shard_map/ppermute | solution.py:22

commit v2 on v0

v2 whole, which is shorter than its diff:
```python
import functools

import jax
import jax.numpy as jnp
from jax import lax
from jax.experimental import pallas as pl
from jax.experimental.pallas import tpu as pltpu
from jax.sharding import Mesh, PartitionSpec as P

BF = jnp.bfloat16
F32 = jnp.float32
Z, Y, X = 8, 8, 4
YP = 2
YQ = Y // YP
TOK, PAD = 30, 32
HALF = PAD // 2
SIDE = Z * HALF
ALL = 2 * SIDE
FS, FT = 64, 128
HY = Y // 2
PART = HY * (FT + FS)
D_S, D_T = X * Y * FS, X * Y * FT
NT = (((1,), (1,)), ((), ()))


def call(kernel, out, *args, scratch=(), mib=24, flops=0, scalars=0, anywhere=0, cheap=False):
    specs = [pl.BlockSpec(memory_space=pltpu.SMEM)] * scalars
    specs += [pl.BlockSpec(memory_space=pltpu.VMEM)] * (len(args) - scalars - anywhere)
    specs += [pl.BlockSpec(memory_space=pl.ANY)] * anywhere
    outs = jax.tree.map(lambda o: pl.BlockSpec(memory_space=pltpu.VMEM), out)
    size = sum(a.size * a.dtype.itemsize for a in args) + sum(
        o.size * o.dtype.itemsize for o in jax.tree.leaves(out)
    )
    return pl.pallas_call(
        kernel,
        out_shape=out,
        in_specs=specs,
        out_specs=outs,
        scratch_shapes=scratch,
        compiler_params=pltpu.CompilerParams(vmem_limit_bytes=mib << 20),
        cost_estimate=pl.CostEstimate(flops=flops, bytes_accessed=0 if cheap else size, transcendentals=0),
    )(*args)


def array(shape, dtype):
    return jax.ShapeDtypeStruct(shape, dtype)


def message_kernel(s_any, t_any, o_ref, s_in, t_in, s_pad, t_pad, sems):
    copies = [
        pltpu.make_async_copy(s_any, s_in, sems.at[0]),
        pltpu.make_async_copy(t_any, t_in, sems.at[1]),
    ]
    for c in copies:
        c.start()
    s_pad[...] = jnp.zeros_like(s_pad)
    t_pad[...] = jnp.zeros_like(t_pad)
    for c in copies:
        c.wait()
    s_pad[0:TOK, :] = s_in[...].astype(F32)
    t_pad[0:TOK, :] = t_in[...].astype(F32)
    s = jnp.concatenate([s_pad[0:HALF, :], s_pad[HALF:PAD, :]], axis=1).astype(BF)
    both = jnp.concatenate([t_pad[...].astype(BF), s], axis=0)
    for i in range(Z * Y):
        o_ref[i] = both


def block_kernel(g_ref, lo_ref, hi_ref):
    for y in range(Y):
        o_ref = lo_ref if y < HY else hi_ref
        row = (y % HY) * FT
        for h in range(2):
            t = g_ref[:, y, h * HALF : (h + 1) * HALF, :].reshape(SIDE, FT)
            o_ref[row : row + FT, h * SIDE : (h + 1) * SIDE] = t.T
        s = g_ref[:, y, PAD : PAD + HALF, :].reshape(SIDE, 2 * FS).T
        row = HY * FT + (y % HY) * FS
        for h in range(2):
            o_ref[row : row + FS, h * SIDE : (h + 1) * SIDE] = s[h * FS : (h + 1) * FS]


def merged(parts):
    n = parts.shape[0]
    m = parts[0, 0:2]
    for i in range(1, n):
        m = jnp.maximum(m, parts[i, 0:2])
    total = jnp.zeros_like(m)
    cross = jnp.zeros((1, m.shape[1]), F32)
    for i in range(n):
        w = jnp.exp(parts[i, 0:2] - m)
        total = total + w * parts[i, 2:4]
        cross = cross + w[0:1] * parts[i, 4:5]
    return m, total, cross


def rows_of(m, total, cross):
    return jnp.concatenate([m, total, cross, jnp.zeros((3, m.shape[1]), F32)], axis=0)


def early_kernel(x_ref, *refs):
    s_heads, t_heads = refs[0:2], refs[2:4]
    blocks = refs[4:10]
    ls_ref, lt_ref, far_s, far_t, full_t, full_s, sems = refs[10:]
    xi = x_ref[0]
    far = lax.rem(xi + 2, X)
    parts = []
    for i, step in enumerate((0, 1, 3)):
        x = lax.rem(xi + step, X)
        for y in range(Y):
            ref = blocks[2 * i + y // HY]
            row = (y % HY) * FT
            at = pl.multiple_of((y * X + x) * FT, FT)
            parts.append((ref.at[row : row + FT, :], full_t.at[pl.ds(at, FT), :]))
            row = HY * FT + (y % HY) * FS
            at = pl.multiple_of((y * X + x) * FS, FS)
            parts.append((ref.at[row : row + FS, :], full_s.at[pl.ds(at, FS), :]))
    moves = [pltpu.make_async_copy(src, dst, sems.at[i]) for i, (src, dst) in enumerate(parts)]
    for c in moves:
        c.start()
    parts = []
    for b in range(2):
        for y in range(Y):
            cols = slice(y * FT, (y + 1) * FT)
            at = pl.multiple_of((y * X + far) * FT, FT)
            parts.append((t_heads[b].at[:, pl.ds(at, FT)], far_t.at[b, :, cols]))
            at = pl.multiple_of((y * X + far // 2 * 2) * FS, FT)
            parts.append((s_heads[b].at[:, pl.ds(at, FT)], far_s.at[b, :, cols]))
    first = len(moves)
    later = [pltpu.make_async_copy(src, dst, sems.at[first + i]) for i, (src, dst) in enumerate(parts)]
    for c in later:
        c.start()
    for y in range(Y):
        at = pl.multiple_of((y * X + far) * FT, FT)
        full_t[pl.ds(at, FT), :] = jnp.zeros((FT, ALL), BF)
        at = pl.multiple_of((y * X + far) * FS, FS)
        full_s[pl.ds(at, FS), :] = jnp.zeros((FS, ALL), BF)
    for c in moves:
        c.wait()
    for b in range(2):
        ls_ref[b] = jnp.dot(s_heads[b][...], full_s[...], preferred_element_type=F32)
        lt_ref[b] = jnp.dot(t_heads[b][...], full_t[...], preferred_element_type=F32)
    for c in later:
        c.wait()


def late_kernel(x_ref, lo_ref, hi_ref, far_s, far_t, ls_in, lt_in, ls_ref, lt_ref, stat_ref, rows_s, rows_t):
    odd = lax.rem(x_ref[0], 2)
    rows_s[...] = jnp.zeros_like(rows_s)
    for y in range(Y):
        ref = (lo_ref, hi_ref)[y // HY]
        rows_t[y * FT : (y + 1) * FT, :] = ref[(y % HY) * FT : (y % HY + 1) * FT, :]
        row = HY * FT + (y % HY) * FS
        at = pl.multiple_of(y * FT + odd * FS, FS)
        rows_s[pl.ds(at, FS), :] = ref[row : row + FS, :]
    for b in range(2):
        lt_ref[b] = lt_in[b] + jnp.dot(far_t[b], rows_t[...], preferred_element_type=F32)
        ls_ref[b] = ls_in[b] + jnp.dot(far_s[b], rows_s[...], preferred_element_type=F32)
    mt = jnp.maximum(jnp.max(lt_ref[0], axis=0, keepdims=True), jnp.max(lt_ref[1], axis=0, keepdims=True))
    ms = jnp.maximum(jnp.max(ls_ref[0], axis=0, keepdims=True), jnp.max(ls_ref[1], axis=0, keepdims=True))
    sums = [0.0, 0.0, 0.0]
    for b in range(2):
        lt, ls = lt_ref[b], ls_ref[b]
        et = jnp.exp(lt - mt)
        new = (et, jnp.exp(ls - ms), et * (lt - ls))
        sums = [a + jnp.sum(v, axis=0, keepdims=True) for a, v in zip(sums, new)]
    stat = jnp.concatenate([mt, ms] + sums + [jnp.zeros((3, ALL), F32)], axis=0)
    for i in range(Y * X):
        stat_ref[i] = stat


def fill_kernel(x_ref, *refs):
    blocks, o_ref, sems = refs[0:8], refs[9], refs[10]
    moves = []
    for step in range(X):
        x = lax.rem(x_ref[0] + step, X)
        for y in range(Y):
            ref = blocks[2 * step + y // HY]
            row = HY * FT + (y % HY) * FS
            at = pl.multiple_of((y * X + x) * FS, FS)
            dst = o_ref.at[pl.ds(at, FS), :]
            moves.append(pltpu.make_async_copy(ref.at[row : row + FS, :], dst, sems.at[step * Y + y]))
            moves[-1].start()
    for c in moves:
        c.wait()


def merge_kernel(p_ref, o_ref):
    stat = rows_of(*merged(p_ref))
    for i in range(Z):
        o_ref[i] = stat


def grads_kernel(p_ref, ls_ref, lt_ref, s0_ref, s1_ref, g_ref, by_ypx_ref, kl_ref, terms):
    m, total, cross = merged(p_ref)
    lse = m + jnp.log(total)
    lse_t, lse_s = lse[0:1], lse[1:2]
    kl = cross / total[0:1] - lse_t + lse_s
    lane = lax.broadcasted_iota(jnp.int32, (1, ALL), 1)
    padding = (lane >= SIDE) & ((lane & (HALF - 1)) >= TOK - HALF)
    kl_ref[...] = jnp.broadcast_to(jnp.sum(jnp.where(padding, 0.0, kl), axis=1, keepdims=True), kl_ref.shape)
    for b, head in enumerate((s0_ref, s1_ref)):
        g = (jnp.exp(ls_ref[b] - lse_s) - jnp.exp(lt_ref[b] - lse_t)).astype(BF)
        g_ref[b] = g
        part = lax.dot_general(g, head[...], (((0,), (0,)), ((), ())), preferred_element_type=F32)
        terms[...] = part if b == 0 else terms[...] + part
    for yp in range(YP):
        for x in range(X):
            for q in range(YQ // 2):
                ys = [(2 * q + i) * YP + yp for i in range(2)]
                pair = [terms[:, (y * X + x) * FS : (y * X + x + 1) * FS] for y in ys]
                by_ypx_ref[yp * X + x, :, q * 2 * FS : (q + 1) * 2 * FS] = jnp.concatenate(pair, axis=1).astype(BF)


def thirds(v):
    hi = v.astype(BF)
    mid = (v - hi.astype(F32)).astype(BF)
    return hi, mid, (v - hi.astype(F32) - mid.astype(F32)).astype(BF)


def sent_kernel(g_ref, full_s, kl_ref, o_ref):
    o_ref[:, 0:D_S] = lax.dot_general(g_ref[1], full_s[...], NT, preferred_element_type=F32).astype(BF)
    lane = lax.broadcasted_iota(jnp.int32, (1, 128), 1)
    row = jnp.zeros((1, 128), F32)
    for i, v in enumerate(thirds(kl_ref[0:1, :])):
        row = jnp.where(lane == i, v.astype(F32), row)
    o_ref[:, D_S : D_S + 128] = jnp.broadcast_to(row, (o_ref.shape[0], 128)).astype(BF)


def kept_kernel(g_ref, full_s, kl_ref, arrived, o_ref, loss_ref):
    kept = lax.dot_general(g_ref[0], full_s[...], NT, preferred_element_type=F32)
    o_ref[...] = (kept + arrived[:, 0:D_S].astype(F32)).astype(BF)
    hi, mid, lo = [v.astype(F32) for v in thirds(kl_ref[0:1, 0:1])]
    other = arrived[0:16, D_S : D_S + 128].astype(F32)[0:1]
    there = other[:, 0:1] + other[:, 1:2] + other[:, 2:3]
    loss_ref[...] = (hi + mid + lo + there) / (2 * Z * TOK)


def pack_kernel(r_ref, _, o_ref):
    row = r_ref[0].astype(F32)
    for i in range(1, YP * X):
        row = row + r_ref[i].astype(F32)
    for z in range(Z):
        sides = [row[h * SIDE + z * HALF : h * SIDE + (z + 1) * HALF] for h in range(2)]
        for yq in range(YQ):
            pair = [v[:, yq * FS : (yq + 1) * FS] for v in sides]
            o_ref[z * YQ + yq] = jnp.concatenate(pair, axis=1).astype(BF)


def last_kernel(r_ref, o_ref):
    total = jnp.sum(r_ref[...].astype(F32), axis=0)
    o_ref[0:HALF, :] = total[:, 0:FS]
    o_ref[HALF:TOK, :] = total[0 : TOK - HALF, FS : 2 * FS]


def exchange(v, axes):
    return lax.all_to_all(v, axes, 0, 0, tiled=True)


def swap(v):
    return lax.ppermute(v, "core", [(0, 1), (1, 0)])


def along_x(v, step):
    return lax.ppermute(v, "x", [(i, (i + step) % X) for i in range(X)])


def local(student_hidden, teacher_hidden, student_head, teacher_head):
    rows = student_head.shape[0]
    xi = lax.axis_index("x").reshape(1)
    s_heads = [student_head, swap(student_head)]
    t_heads = [teacher_head, swap(teacher_head)]

    message = call(
        message_kernel,
        array((Z * Y, PAD + HALF, FT), BF),
        student_hidden,
        teacher_hidden,
        anywhere=2,
        mib=60,
        scratch=[
            pltpu.VMEM((TOK, FS), BF),
            pltpu.VMEM((TOK, FT), BF),
            pltpu.VMEM((PAD, FS), F32),
            pltpu.VMEM((PAD, FT), F32),
            pltpu.SemaphoreType.DMA((2,)),
        ],
    )
    near = exchange(message, ("z", "yq", "yp")).reshape(Z, Y, PAD + HALF, FT)
    part = array((PART, ALL), BF)
    own = call(block_kernel, (part, part), near)
    before = [along_x(v, 1) for v in own]
    after = [along_x(v, -1) for v in own]
    far = [along_x(before[0], 1), along_x(after[1], -1)]

    logit = array((2, rows, ALL), F32)
    far_cols = array((2, rows, Y * FT), BF)
    ls, lt, far_s, far_t = call(
        early_kernel,
        (logit, logit, far_cols, far_cols),
        xi,
        *s_heads,
        *t_heads,
        *own,
        *after,
        *before,
        scalars=1,
        anywhere=6,
        mib=16,
        cheap=True,
        scratch=[
            pltpu.VMEM((D_T, ALL), BF),
            pltpu.VMEM((D_S, ALL), BF),
            pltpu.SemaphoreType.DMA((10 * Y,)),
        ],
    )
    ls, lt, stat = call(
        late_kernel,
        (logit, logit, array((Y * X, 8, ALL), F32)),
        xi,
        *far,
        far_s,
        far_t,
        ls,
        lt,
        scalars=1,
        scratch=[pltpu.VMEM((Y * FT, ALL), BF), pltpu.VMEM((Y * FT, ALL), BF)],
        flops=8 * rows * ALL * Y * FT,
    )
    stat = exchange(stat, ("yq", "yp", "x"))
    stat = call(merge_kernel, array((Z, 8, ALL), F32), stat)
    stat = exchange(stat, "z")
    grads, by_ypx, kl = call(
        grads_kernel,
        (array((2, rows, ALL), BF), array((YP * X, ALL, YQ * FS), BF), array((8, 128), F32)),
        stat,
        ls,
        lt,
        *s_heads,
        scratch=[pltpu.VMEM((ALL, D_S), F32)],
        flops=4 * rows * ALL * D_S,
    )
    full_s = call(
        fill_kernel,
        array((D_S, ALL), BF),
        xi,
        *own,
        *after,
        *far,
        *before,
        kl,
        scalars=1,
        anywhere=9,
        scratch=[pltpu.SemaphoreType.DMA((X * Y,))],
    )
    sent = call(sent_kernel, array((rows, D_S + 128), BF), grads, full_s, kl, flops=2 * rows * ALL * D_S)
    packed = call(
        pack_kernel, array((Z * YQ, HALF, 2 * FS), BF), exchange(by_ypx, ("yp", "x")), sent, anywhere=1
    )
    hidden_grad = call(last_kernel, array((TOK, FS), F32), exchange(packed, ("z", "yq")))
    head_grad, loss = call(
        kept_kernel,
        (array((rows, D_S), BF), array((1, 1), F32)),
        grads,
        full_s,
        kl,
        swap(sent),
        flops=2 * rows * ALL * D_S,
    )
    return (loss.reshape(()), hidden_grad, head_grad)


def solution(mesh):
    fine = Mesh(mesh.devices.reshape(Z, 2, YQ, YP, X), ("z", "core", "yq", "yp", "x"))
    rows, cols = ("z", "core"), ("yq", "yp", "x")
    return jax.shard_map(
        local,
        mesh=fine,
        in_specs=(P(rows, cols), P(rows, cols), P(rows + cols, None), P(rows + cols, None)),
        out_specs=(P(), P(rows, cols), P(rows + cols, None)),
        check_vma=False,
    )
```

time: 1840 us -> 145 us (0.08)
  the two profiles are of different devices: /device:TPU:1 before, /device:TPU:8 now
where the time goes in v2:
time: 145 us; the launch traced here: 144 us
  starting transfers between devices  51.1 us (35%)
  waiting for transfers between devices  41.3 us (28%)
  blocking collectives  29.2 us (20%)
  Pallas kernels  18.4 us (13%)
  local copies, waits for them, and re-layouts  3.2 us (2%)
    all_to_all x3, waiting for transfers between devices, exchange(): return lax.all_to_all(v, axes, 0, 0, tiled=True)  35.2 us
    all_to_all x2, blocking collectives, exchange(): return lax.all_to_all(v, axes, 0, 0, tiled=True)  29.2 us
    all_to_all x3, starting transfers between devices, exchange(): return lax.all_to_all(v, axes, 0, 0, tiled=True)  24.9 us
    ppermute x6, starting transfers between devices, along_x(): return lax.ppermute(v, 'x', [(i, (i + step) % X) for i in range(X)])  19.9 us
    pallas_call x11, Pallas kernels, call(): pl.pallas_call(kernel, out_shape=out, in_specs=specs, out_specs=outs, scr...  18.4 us
    ppermute x3, starting transfers between devices, swap(): return lax.ppermute(v, 'core', [(0, 1), (1, 0)])  6.25 us
    ppermute x6, waiting for transfers between devices, along_x(): return lax.ppermute(v, 'x', [(i, (i + step) % X) for i in range(X)])  6.09 us
    unnamed x8, local copies, waits for them, and re-layouts  3.2 us
  transfers between devices with their start and end apart: 12, of which 5 were waited for; matrix products, arithmetic and copies ran while one was open for 0% of the time, Pallas kernels for 9%

profile of v2, /device:TPU:8, one launch (start us, length us, event | category | flops | bytes accessed | tf_op | source)
XLA Modules:
  0.0 144.1 jit_solution(9187093213408943474)
XLA Ops:
  0.6 0.0 copy-start
  0.6 1.8 %shard_map.67 = bf16[64,48,128]{2,1,0:T(8,128)(2,1)} custom-call(bf16[30,64]{1,0:T(8,128)(2,1)} %s_any.1, bf16[30,128]{1,0:T(8,128)(2,1)} %t_any.1), custom_call_target="tpu_custom_call" | custom-call | bytes 797952 | tf_op jit(solution)/shard_map/pallas_call | solution.py:34
  2.5 16.6 %all-to-all-start = ((bf16[64,48,128]{2,1,0:T(8,128)(2,1)}), bf16[64,48,128]{2,1,0:T(8,128)(2,1)S(1)}, u32[]{:S(2)}, u32[]{:S(2)}) async-start(bf16[64,48,128]{2,1,0:T(8,128)(2,1)} %shard_map.67), calls=%async_computation | async-start | bytes 1572864 | tf_op jit(solution)/shard_map/all_to_all | solution.py:255
  19.1 1.9 %collective-permute-start.5 = (bf16[250,4096]{1,0:T(8,128)(2,1)}, bf16[250,4096]{1,0:T(8,128)(2,1)}, u32[]{:S(2)}, u32[]{:S(2)}) collective-permute-start(bf16[250,4096]{1,0:T(8,128)(2,1)} %refs_2_.1), channel_id=1, source_target_pairs={{0,32},{32,0},{1,33},{33,1},{2,34},{34,2},{3,35},{35,3},{4,36},{36... | collective-permute-start | bytes 6144008 | tf_op jit(solution)/shard_map/ppermute | solution.py:259
  21.0 0.0 copy-done
  21.0 2.4 %collective-permute-start.4 = (bf16[250,2048]{1,0:T(8,128)(2,1)S(1)}, bf16[250,2048]{1,0:T(8,128)(2,1)S(1)}, u32[]{:S(2)}, u32[]{:S(2)}) collective-permute-start(bf16[250,2048]{1,0:T(8,128)(2,1)S(1)} %copy-done), channel_id=1, source_target_pairs={{0,32},{32,0},{1,33},{33,1},{2,34},{34,2},{3,35},{35,3},{4,36},{36... | collective-permute-start | bytes 3072008 | tf_op jit(solution)/shard_map/ppermute | solution.py:259
  23.4 19.6 %all-to-all-done = bf16[64,48,128]{2,1,0:T(8,128)(2,1)S(1)} async-done(((bf16[64,48,128]{2,1,0:T(8,128)(2,1)}), bf16[64,48,128]{2,1,0:T(8,128)(2,1)S(1)}, u32[]{:S(2)}, u32[]{:S(2)}) %all-to-all-start) | async-done | bytes 786464 | tf_op jit(solution)/shard_map/all_to_all | solution.py:255
  43.0 1.0 shard_map.68
  44.0 3.4 %collective-permute-start = (bf16[768,256]{1,0:T(8,128)(2,1)S(1)}, bf16[768,256]{1,0:T(8,128)(2,1)S(1)}, u32[]{:S(2)}, u32[]{:S(2)}) collective-permute-start(bf16[768,256]{1,0:T(8,128)(2,1)S(1)} %get-tuple-element.17.refs_4_.refs_0_), channel_id=1, source_target_pairs={{0,1},{1,2},{2,3},{3,0},{4,5},{5,6},{6,7},{7,4},{8,9},{9,10},{10,1... | collective-permute-start | bytes 1179656 | tf_op jit(solution)/shard_map/ppermute | solution.py:263
  47.4 3.7 %collective-permute-start.2 = (bf16[768,256]{1,0:T(8,128)(2,1)}, bf16[768,256]{1,0:T(8,128)(2,1)S(1)}, u32[]{:S(2)}, u32[]{:S(2)}) collective-permute-start(bf16[768,256]{1,0:T(8,128)(2,1)} %get-tuple-element.18.refs_5_.refs_1_), channel_id=1, source_target_pairs={{0,3},{1,0},{2,1},{3,2},{4,7},{5,4},{6,5},{7,6},{8,11},{9,8},{10,9... | collective-permute-start | bytes 1179656 | tf_op jit(solution)/shard_map/ppermute | solution.py:263
  51.1 3.5 %collective-permute-start.6 = (bf16[768,256]{1,0:T(8,128)(2,1)S(1)}, bf16[768,256]{1,0:T(8,128)(2,1)}, u32[]{:S(2)}, u32[]{:S(2)}) collective-permute-start(bf16[768,256]{1,0:T(8,128)(2,1)S(1)} %get-tuple-element.17.refs_4_.refs_0_), channel_id=1, source_target_pairs={{0,3},{1,0},{2,1},{3,2},{4,7},{5,4},{6,5},{7,6},{8,11},{9,8},{10,9... | collective-permute-start | bytes 1179656 | tf_op jit(solution)/shard_map/ppermute | solution.py:263
  54.6 0.0 collective-permute-done.4.refs_1_.s1_ref
  54.6 2.4 %collective-permute-start.7 = (bf16[768,256]{1,0:T(8,128)(2,1)}, bf16[768,256]{1,0:T(8,128)(2,1)}, u32[]{:S(2)}, u32[]{:S(2)}) collective-permute-start(bf16[768,256]{1,0:T(8,128)(2,1)} %get-tuple-element.18.refs_5_.refs_1_), channel_id=1, source_target_pairs={{0,1},{1,2},{2,3},{3,0},{4,5},{5,6},{6,7},{7,4},{8,9},{9,10},{10,1... | collective-permute-start | bytes 1179656 | tf_op jit(solution)/shard_map/ppermute | solution.py:263
  57.0 0.0 collective-permute-done.refs_8_.refs_6_
  57.0 2.2 %collective-permute-start.1 = (bf16[768,256]{1,0:T(8,128)(2,1)S(1)}, bf16[768,256]{1,0:T(8,128)(2,1)}, u32[]{:S(2)}, u32[]{:S(2)}) collective-permute-start(bf16[768,256]{1,0:T(8,128)(2,1)S(1)} %collective-permute-done.refs_8_.refs_6_), channel_id=1, source_target_pairs={{0,1},{1,2},{2,3},{3,0},{4,5},{5,6},{6,7},{7,4},{8,9},{9,10},{10,1... | collective-permute-start | bytes 1179656 | tf_op jit(solution)/shard_map/ppermute | solution.py:263
  59.2 2.4 %collective-permute-done.2.refs_7_.refs_3_ = bf16[768,256]{1,0:T(8,128)(2,1)S(1)} collective-permute-done((bf16[768,256]{1,0:T(8,128)(2,1)}, bf16[768,256]{1,0:T(8,128)(2,1)S(1)}, u32[]{:S(2)}, u32[]{:S(2)}) %collective-permute-start.2) | collective-permute-done | bytes 393248 | tf_op jit(solution)/shard_map/ppermute | solution.py:263
  61.6 4.9 %collective-permute-start.3 = (bf16[768,256]{1,0:T(8,128)(2,1)S(1)}, bf16[768,256]{1,0:T(8,128)(2,1)}, u32[]{:S(2)}, u32[]{:S(2)}) collective-permute-start(bf16[768,256]{1,0:T(8,128)(2,1)S(1)} %collective-permute-done.2.refs_7_.refs_3_), channel_id=1, source_target_pairs={{0,3},{1,0},{2,1},{3,2},{4,7},{5,4},{6,5},{7,6},{8,11},{9,8},{10,9... | collective-permute-start | bytes 1179656 | tf_op jit(solution)/shard_map/ppermute | solution.py:263
  66.4 3.7 %collective-permute-done.6.refs_6_.refs_2_ = bf16[768,256]{1,0:T(8,128)(2,1)} collective-permute-done((bf16[768,256]{1,0:T(8,128)(2,1)S(1)}, bf16[768,256]{1,0:T(8,128)(2,1)}, u32[]{:S(2)}, u32[]{:S(2)}) %collective-permute-start.6) | collective-permute-done | bytes 393248 | tf_op jit(solution)/shard_map/ppermute | solution.py:263
  70.1 0.0 collective-permute-done.7.refs_9_.refs_7_
  70.1 0.0 collective-permute-done.5.refs_3_
  70.1 0.0 copy-start.1
  70.1 1.6 %copy-done.1 = bf16[250,4096]{1,0:T(8,128)(2,1)S(1)} copy-done((bf16[250,4096]{1,0:T(8,128)(2,1)S(1)}, bf16[250,4096]{1,0:T(8,128)(2,1)}, u32[]{:S(2)}) %copy-start.1) | copy-done | bytes 2048024
  71.7 6.7 %shard_map.69 = (f32[2,250,256]{2,1,0:T(8,128)S(1)}, f32[2,250,256]{2,1,0:T(8,128)S(1)}, bf16[2,250,1024]{2,1,0:T(8,128)(2,1)S(1)}, bf16[2,250,1024]{2,1,0:T(8,128)(2,1)S(1)}) custom-call(s32[1]{0:T(128)} %bitcast.x_ref, bf16[250,2048]{1,0:T(8,128)(2,1)S(1)} %copy-done, bf16[250,2048]{1,0:T(8,128)(2,1)S(1)} %collective-permute-done.4.refs_1_.s1_ref, ...), custom_call_target="tpu_custom_call" | custom-call | tf_op jit(solution)/shard_map/pallas_call | solution.py:34
  78.4 0.0 collective-permute-done.1.lo_ref.refs_4_
  78.4 0.0 collective-permute-done.3.hi_ref.refs_5_
  78.4 2.1 %shard_map.70 = (f32[2,250,256]{2,1,0:T(8,128)S(1)}, f32[2,250,256]{2,1,0:T(8,128)S(1)}, f32[32,8,256]{2,1,0:T(8,128)S(1)}) custom-call(s32[1]{0:T(128)} %bitcast.x_ref, bf16[768,256]{1,0:T(8,128)(2,1)} %collective-permute-done.1.lo_ref.refs_4_, bf16[768,256]{1,0:T(8,128)(2,1)} %collective-permute-done.3.hi_ref.refs_5_, ...), custom_call_target="tpu_custom_call" | custom-call | flops 524288000 | bytes 5144580 | tf_op jit(solution)/shard_map/pallas_call | solution.py:34
  80.6 18.4 %all_to_all.25.p_ref = f32[32,8,256]{2,1,0:T(8,128)S(1)} all-to-all(f32[32,8,256]{2,1,0:T(8,128)S(1)} %get-tuple-element.23), channel_id=1, replica_groups=mesh['z'=8,'core'=2,'yq'=4,'yp'=2,'x'=4] {'yq','yp','x'}, dimensions={0} | all-to-all | bytes 524288 | tf_op jit(solution)/shard_map/all_to_all | solution.py:255
  99.0 0.1 shard_map.71
  99.1 10.8 %all_to_all.26.p_ref = f32[8,8,256]{2,1,0:T(8,128)S(1)} all-to-all(f32[8,8,256]{2,1,0:T(8,128)S(1)} %shard_map.71), channel_id=1, replica_groups=mesh['z'=8,'core'=2,'yq'=4,'yp'=2,'x'=4] {'z'}, dimensions={0} | all-to-all | bytes 131072 | tf_op jit(solution)/shard_map/all_to_all | solution.py:255
  109.9 0.9 shard_map.72
  110.8 0.0 copy-start.2
  110.8 1.0 copy-done.2
  111.8 4.5 %all-to-all-start.3 = ((bf16[8,256,256]{2,1,0:T(8,128)(2,1)}), bf16[8,256,256]{2,1,0:T(8,128)(2,1)S(1)}, u32[]{:S(2)}, u32[]{:S(2)}) async-start(bf16[8,256,256]{2,1,0:T(8,128)(2,1)} %copy-done.2), calls=%async_computation.3 | async-start | bytes 2097152 | tf_op jit(solution)/shard_map/all_to_all | solution.py:255
  116.2 1.7 %shard_map.73.full_s = bf16[2048,256]{1,0:T(8,128)(2,1)S(1)} custom-call(s32[1]{0:T(128)} %bitcast.x_ref, bf16[768,256]{1,0:T(8,128)(2,1)S(1)} %get-tuple-element.17.refs_4_.refs_0_, bf16[768,256]{1,0:T(8,128)(2,1)} %get-tuple-element.18.refs_5_.refs_1_, bf16[768,256]{1,0:T(8,128)(2,1)} %collective-permute-done.6.refs_6_.refs_2_, ...), custom_call_target="tpu_custom_call" | custom-call | bytes 4198404 | tf_op jit(solution)/shard_map/pallas_call | solution.py:34
  117.9 0.5 shard_map.74._
  118.4 1.9 %collective-permute-start.8 = (bf16[250,2176]{1,0:T(8,128)(2,1)S(1)}, bf16[250,2176]{1,0:T(8,128)(2,1)}, u32[]{:S(2)}, u32[]{:S(2)}) collective-permute-start(bf16[250,2176]{1,0:T(8,128)(2,1)S(1)} %shard_map.74._), channel_id=1, source_target_pairs={{0,32},{32,0},{1,33},{33,1},{2,34},{34,2},{3,35},{35,3},{4,36},{36... | collective-permute-start | bytes 3264008 | tf_op jit(solution)/shard_map/ppermute | solution.py:259
  120.3 5.9 %all-to-all-done.3.r_ref = bf16[8,256,256]{2,1,0:T(8,128)(2,1)S(1)} async-done(((bf16[8,256,256]{2,1,0:T(8,128)(2,1)}), bf16[8,256,256]{2,1,0:T(8,128)(2,1)S(1)}, u32[]{:S(2)}, u32[]{:S(2)}) %all-to-all-start.3) | async-done | bytes 1048608 | tf_op jit(solution)/shard_map/all_to_all | solution.py:255
  126.3 0.2 shard_map.76
  126.5 0.0 copy-start.3
  126.5 0.6 copy-done.3
  127.1 3.8 %all-to-all-start.4 = ((bf16[32,16,128]{2,1,0:T(8,128)(2,1)}), bf16[32,16,128]{2,1,0:T(8,128)(2,1)S(1)}, u32[]{:S(2)}, u32[]{:S(2)}) async-start(bf16[32,16,128]{2,1,0:T(8,128)(2,1)} %copy-done.3), calls=%async_computation.4 | async-start | bytes 262144 | tf_op jit(solution)/shard_map/all_to_all | solution.py:255
  131.0 0.0 collective-permute-done.8.arrived
  131.0 2.7 %shard_map.75 = (bf16[250,2048]{1,0:T(8,128)(2,1)}, f32[1,1]{1,0:T(1,128)}) custom-call(bf16[2,250,256]{2,1,0:T(8,128)(2,1)S(1)} %get-tuple-element.26.g_ref, bf16[2048,256]{1,0:T(8,128)(2,1)S(1)} %shard_map.73.full_s, f32[8,128]{1,0:T(8,128)S(1)} %get-tuple-element.27.refs_8_.kl_ref, bf16[250,2176]{1,0:T(8,128)(2,1)} %collective-permute-done.8.arrived), custom_call_target="tpu_custom_call" | custom-call | flops 262144000 | bytes 3420676 | tf_op jit(solution)/shard_map/pallas_call | solution.py:34
  133.7 9.7 %all-to-all-done.4.r_ref = bf16[32,16,128]{2,1,0:T(8,128)(2,1)S(1)} async-done(((bf16[32,16,128]{2,1,0:T(8,128)(2,1)}), bf16[32,16,128]{2,1,0:T(8,128)(2,1)S(1)}, u32[]{:S(2)}, u32[]{:S(2)}) %all-to-all-start.4) | async-done | bytes 131104 | tf_op jit(solution)/shard_map/all_to_all | solution.py:255
  143.4 0.7 shard_map.77
Async XLA Ops:
  0.6 20.4 %copy-start = (bf16[250,2048]{1,0:T(8,128)(2,1)S(1)}, bf16[250,2048]{1,0:T(8,128)(2,1)}, u32[]{:S(2)}) copy-start(bf16[250,2048]{1,0:T(8,128)(2,1)} %s0_ref.1) | copy-start | bytes 3072004
  2.5 40.6 %all-to-all-start = ((bf16[64,48,128]{2,1,0:T(8,128)(2,1)}), bf16[64,48,128]{2,1,0:T(8,128)(2,1)S(1)}, u32[]{:S(2)}, u32[]{:S(2)}) async-start(bf16[64,48,128]{2,1,0:T(8,128)(2,1)} %shard_map.67), calls=%async_computation | async-start | bytes 1572864 | tf_op jit(solution)/shard_map/all_to_all | solution.py:255
  19.1 51.1 %collective-permute-start.5 = (bf16[250,4096]{1,0:T(8,128)(2,1)}, bf16[250,4096]{1,0:T(8,128)(2,1)}, u32[]{:S(2)}, u32[]{:S(2)}) collective-permute-start(bf16[250,4096]{1,0:T(8,128)(2,1)} %refs_2_.1), channel_id=1, source_target_pairs={{0,32},{32,0},{1,33},{33,1},{2,34},{34,2},{3,35},{35,3},{4,36},{36... | collective-permute-start | bytes 6144008 | tf_op jit(solution)/shard_map/ppermute | solution.py:259
  21.0 33.6 %collective-permute-start.4 = (bf16[250,2048]{1,0:T(8,128)(2,1)S(1)}, bf16[250,2048]{1,0:T(8,128)(2,1)S(1)}, u32[]{:S(2)}, u32[]{:S(2)}) collective-permute-start(bf16[250,2048]{1,0:T(8,128)(2,1)S(1)} %copy-done), channel_id=1, source_target_pairs={{0,32},{32,0},{1,33},{33,1},{2,34},{34,2},{3,35},{35,3},{4,36},{36... | collective-permute-start | bytes 3072008 | tf_op jit(solution)/shard_map/ppermute | solution.py:259
  44.0 12.9 %collective-permute-start = (bf16[768,256]{1,0:T(8,128)(2,1)S(1)}, bf16[768,256]{1,0:T(8,128)(2,1)S(1)}, u32[]{:S(2)}, u32[]{:S(2)}) collective-permute-start(bf16[768,256]{1,0:T(8,128)(2,1)S(1)} %get-tuple-element.17.refs_4_.refs_0_), channel_id=1, source_target_pairs={{0,1},{1,2},{2,3},{3,0},{4,5},{5,6},{6,7},{7,4},{8,9},{9,10},{10,1... | collective-permute-start | bytes 1179656 | tf_op jit(solution)/shard_map/ppermute | solution.py:263
  47.4 14.2 %collective-permute-start.2 = (bf16[768,256]{1,0:T(8,128)(2,1)}, bf16[768,256]{1,0:T(8,128)(2,1)S(1)}, u32[]{:S(2)}, u32[]{:S(2)}) collective-permute-start(bf16[768,256]{1,0:T(8,128)(2,1)} %get-tuple-element.18.refs_5_.refs_1_), channel_id=1, source_target_pairs={{0,3},{1,0},{2,1},{3,2},{4,7},{5,4},{6,5},{7,6},{8,11},{9,8},{10,9... | collective-permute-start | bytes 1179656 | tf_op jit(solution)/shard_map/ppermute | solution.py:263
  51.1 19.0 %collective-permute-start.6 = (bf16[768,256]{1,0:T(8,128)(2,1)S(1)}, bf16[768,256]{1,0:T(8,128)(2,1)}, u32[]{:S(2)}, u32[]{:S(2)}) collective-permute-start(bf16[768,256]{1,0:T(8,128)(2,1)S(1)} %get-tuple-element.17.refs_4_.refs_0_), channel_id=1, source_target_pairs={{0,3},{1,0},{2,1},{3,2},{4,7},{5,4},{6,5},{7,6},{8,11},{9,8},{10,9... | collective-permute-start | bytes 1179656 | tf_op jit(solution)/shard_map/ppermute | solution.py:263
  54.6 15.6 %collective-permute-start.7 = (bf16[768,256]{1,0:T(8,128)(2,1)}, bf16[768,256]{1,0:T(8,128)(2,1)}, u32[]{:S(2)}, u32[]{:S(2)}) collective-permute-start(bf16[768,256]{1,0:T(8,128)(2,1)} %get-tuple-element.18.refs_5_.refs_1_), channel_id=1, source_target_pairs={{0,1},{1,2},{2,3},{3,0},{4,5},{5,6},{6,7},{7,4},{8,9},{9,10},{10,1... | collective-permute-start | bytes 1179656 | tf_op jit(solution)/shard_map/ppermute | solution.py:263
  57.0 21.4 %collective-permute-start.1 = (bf16[768,256]{1,0:T(8,128)(2,1)S(1)}, bf16[768,256]{1,0:T(8,128)(2,1)}, u32[]{:S(2)}, u32[]{:S(2)}) collective-permute-start(bf16[768,256]{1,0:T(8,128)(2,1)S(1)} %collective-permute-done.refs_8_.refs_6_), channel_id=1, source_target_pairs={{0,1},{1,2},{2,3},{3,0},{4,5},{5,6},{6,7},{7,4},{8,9},{9,10},{10,1... | collective-permute-start | bytes 1179656 | tf_op jit(solution)/shard_map/ppermute | solution.py:263
  61.6 16.8 %collective-permute-start.3 = (bf16[768,256]{1,0:T(8,128)(2,1)S(1)}, bf16[768,256]{1,0:T(8,128)(2,1)}, u32[]{:S(2)}, u32[]{:S(2)}) collective-permute-start(bf16[768,256]{1,0:T(8,128)(2,1)S(1)} %collective-permute-done.2.refs_7_.refs_3_), channel_id=1, source_target_pairs={{0,3},{1,0},{2,1},{3,2},{4,7},{5,4},{6,5},{7,6},{8,11},{9,8},{10,9... | collective-permute-start | bytes 1179656 | tf_op jit(solution)/shard_map/ppermute | solution.py:263
  70.1 1.6 %copy-start.1 = (bf16[250,4096]{1,0:T(8,128)(2,1)S(1)}, bf16[250,4096]{1,0:T(8,128)(2,1)}, u32[]{:S(2)}) copy-start(bf16[250,4096]{1,0:T(8,128)(2,1)} %refs_2_.1) | copy-start | bytes 6144004
  110.8 1.0 copy-start.2
  111.8 14.5 %all-to-all-start.3 = ((bf16[8,256,256]{2,1,0:T(8,128)(2,1)}), bf16[8,256,256]{2,1,0:T(8,128)(2,1)S(1)}, u32[]{:S(2)}, u32[]{:S(2)}) async-start(bf16[8,256,256]{2,1,0:T(8,128)(2,1)} %copy-done.2), calls=%async_computation.3 | async-start | bytes 2097152 | tf_op jit(solution)/shard_map/all_to_all | solution.py:255
  118.4 12.6 %collective-permute-start.8 = (bf16[250,2176]{1,0:T(8,128)(2,1)S(1)}, bf16[250,2176]{1,0:T(8,128)(2,1)}, u32[]{:S(2)}, u32[]{:S(2)}) collective-permute-start(bf16[250,2176]{1,0:T(8,128)(2,1)S(1)} %shard_map.74._), channel_id=1, source_target_pairs={{0,32},{32,0},{1,33},{33,1},{2,34},{34,2},{3,35},{35,3},{4,36},{36... | collective-permute-start | bytes 3264008 | tf_op jit(solution)/shard_map/ppermute | solution.py:259
  126.5 0.6 copy-start.3
  127.1 16.2 %all-to-all-start.4 = ((bf16[32,16,128]{2,1,0:T(8,128)(2,1)}), bf16[32,16,128]{2,1,0:T(8,128)(2,1)S(1)}, u32[]{:S(2)}, u32[]{:S(2)}) async-start(bf16[32,16,128]{2,1,0:T(8,128)(2,1)} %copy-done.3), calls=%async_computation.4 | async-start | bytes 262144 | tf_op jit(solution)/shard_map/all_to_all | solution.py:255

commit v3 on v2

--- a/solution.py
+++ b/solution.py
@@ -97,25 +97,20 @@
 
 
 def early_kernel(x_ref, *refs):
-    s_heads, t_heads = refs[0:2], refs[2:4]
-    blocks = refs[4:10]
+    s_heads, t_heads, blocks = refs[0:2], refs[2:4], refs[4:10]
     ls_ref, lt_ref, far_s, far_t, full_t, full_s, sems = refs[10:]
     xi = x_ref[0]
     far = lax.rem(xi + 2, X)
-    parts = []
     for i, step in enumerate((0, 1, 3)):
         x = lax.rem(xi + step, X)
         for y in range(Y):
             ref = blocks[2 * i + y // HY]
+            row = HY * FT + (y % HY) * FS
+            at = pl.multiple_of((y * X + x) * FS, FS)
+            pltpu.make_async_copy(ref.at[row : row + FS, :], full_s.at[pl.ds(at, FS), :], sems.at[0]).start()
             row = (y % HY) * FT
             at = pl.multiple_of((y * X + x) * FT, FT)
-            parts.append((ref.at[row : row + FT, :], full_t.at[pl.ds(at, FT), :]))
-            row = HY * FT + (y % HY) * FS
-            at = pl.multiple_of((y * X + x) * FS, FS)
-            parts.append((ref.at[row : row + FS, :], full_s.at[pl.ds(at, FS), :]))
-    moves = [pltpu.make_async_copy(src, dst, sems.at[i]) for i, (src, dst) in enumerate(parts)]
-    for c in moves:
-        c.start()
+            pltpu.make_async_copy(ref.at[row : row + FT, :], full_t.at[pl.ds(at, FT), :], sems.at[1]).start()
     parts = []
     for b in range(2):
         for y in range(Y):
@@ -124,8 +119,7 @@
             parts.append((t_heads[b].at[:, pl.ds(at, FT)], far_t.at[b, :, cols]))
             at = pl.multiple_of((y * X + far // 2 * 2) * FS, FT)
             parts.append((s_heads[b].at[:, pl.ds(at, FT)], far_s.at[b, :, cols]))
-    first = len(moves)
-    later = [pltpu.make_async_copy(src, dst, sems.at[first + i]) for i, (src, dst) in enumerate(parts)]
+    later = [pltpu.make_async_copy(src, dst, sems.at[2 + i]) for i, (src, dst) in enumerate(parts)]
     for c in later:
         c.start()
     for y in range(Y):
@@ -133,10 +127,13 @@
         full_t[pl.ds(at, FT), :] = jnp.zeros((FT, ALL), BF)
         at = pl.multiple_of((y * X + far) * FS, FS)
         full_s[pl.ds(at, FS), :] = jnp.zeros((FS, ALL), BF)
-    for c in moves:
-        c.wait()
+    arrived = full_s.at[0 : D_S // X * 3, :]
+    pltpu.make_async_copy(arrived, arrived, sems.at[0]).wait()
     for b in range(2):
         ls_ref[b] = jnp.dot(s_heads[b][...], full_s[...], preferred_element_type=F32)
+    arrived = full_t.at[0 : D_T // X * 3, :]
+    pltpu.make_async_copy(arrived, arrived, sems.at[1]).wait()
+    for b in range(2):
         lt_ref[b] = jnp.dot(t_heads[b][...], full_t[...], preferred_element_type=F32)
     for c in later:
         c.wait()
@@ -168,19 +165,15 @@
 
 
 def fill_kernel(x_ref, *refs):
-    blocks, o_ref, sems = refs[0:8], refs[9], refs[10]
-    moves = []
+    blocks, o_ref, sem = refs[0:8], refs[9], refs[10]
     for step in range(X):
         x = lax.rem(x_ref[0] + step, X)
         for y in range(Y):
             ref = blocks[2 * step + y // HY]
             row = HY * FT + (y % HY) * FS
             at = pl.multiple_of((y * X + x) * FS, FS)
-            dst = o_ref.at[pl.ds(at, FS), :]
-            moves.append(pltpu.make_async_copy(ref.at[row : row + FS, :], dst, sems.at[step * Y + y]))
-            moves[-1].start()
-    for c in moves:
-        c.wait()
+            pltpu.make_async_copy(ref.at[row : row + FS, :], o_ref.at[pl.ds(at, FS), :], sem).start()
+    pltpu.make_async_copy(o_ref, o_ref, sem).wait()
 
 
 def merge_kernel(p_ref, o_ref):
@@ -309,7 +302,7 @@
         scratch=[
             pltpu.VMEM((D_T, ALL), BF),
             pltpu.VMEM((D_S, ALL), BF),
-            pltpu.SemaphoreType.DMA((10 * Y,)),
+            pltpu.SemaphoreType.DMA((2 + 4 * Y,)),
         ],
     )
     ls, lt, stat = call(
@@ -349,7 +342,7 @@
         kl,
         scalars=1,
         anywhere=9,
-        scratch=[pltpu.SemaphoreType.DMA((X * Y,))],
+        scratch=[pltpu.SemaphoreType.DMA],
     )
     sent = call(sent_kernel, array((rows, D_S + 128), BF), grads, full_s, kl, flops=2 * rows * ALL * D_S)
     packed = call(

time: 145 us -> 145 us (level)
  transfers between devices with their start and end apart: 12 -> 12, of which waited for: 5 -> 5; matrix products, arithmetic and copies ran while one was open for 0% -> 0% of each run, Pallas kernels for 9% -> 8%
where the time goes in v3:
time: 145 us; the launch traced here: 144 us
  starting transfers between devices  51.1 us (35%)
  waiting for transfers between devices  41.6 us (29%)
  blocking collectives  29.2 us (20%)
  Pallas kernels  17.8 us (12%)
  local copies, waits for them, and re-layouts  3.2 us (2%)
    all_to_all x3, waiting for transfers between devices, exchange(): return lax.all_to_all(v, axes, 0, 0, tiled=True)  35.5 us
    all_to_all x2, blocking collectives, exchange(): return lax.all_to_all(v, axes, 0, 0, tiled=True)  29.2 us
    all_to_all x3, starting transfers between devices, exchange(): return lax.all_to_all(v, axes, 0, 0, tiled=True)  24.9 us
    ppermute x6, starting transfers between devices, along_x(): return lax.ppermute(v, 'x', [(i, (i + step) % X) for i in range(X)])  19.9 us
    pallas_call x11, Pallas kernels, call(): pl.pallas_call(kernel, out_shape=out, in_specs=specs, out_specs=outs, scr...  17.8 us
    ppermute x3, starting transfers between devices, swap(): return lax.ppermute(v, 'core', [(0, 1), (1, 0)])  6.25 us
    ppermute x6, waiting for transfers between devices, along_x(): return lax.ppermute(v, 'x', [(i, (i + step) % X) for i in range(X)])  6.09 us
    unnamed x8, local copies, waits for them, and re-layouts  3.2 us
  transfers between devices with their start and end apart: 12, of which 5 were waited for; matrix products, arithmetic and copies ran while one was open for 0% of the time, Pallas kernels for 8%

profile of v3, /device:TPU:8, one launch (start us, length us, event | category | flops | bytes accessed | tf_op | source)
XLA Modules:
  0.0 143.7 jit_solution(18167152793937845597)
XLA Ops:
  0.6 0.0 copy-start
  0.6 1.8 %shard_map.67 = bf16[64,48,128]{2,1,0:T(8,128)(2,1)} custom-call(bf16[30,64]{1,0:T(8,128)(2,1)} %s_any.1, bf16[30,128]{1,0:T(8,128)(2,1)} %t_any.1), custom_call_target="tpu_custom_call" | custom-call | bytes 797952 | tf_op jit(solution)/shard_map/pallas_call | solution.py:34
  2.5 16.6 %all-to-all-start = ((bf16[64,48,128]{2,1,0:T(8,128)(2,1)}), bf16[64,48,128]{2,1,0:T(8,128)(2,1)S(1)}, u32[]{:S(2)}, u32[]{:S(2)}) async-start(bf16[64,48,128]{2,1,0:T(8,128)(2,1)} %shard_map.67), calls=%async_computation | async-start | bytes 1572864 | tf_op jit(solution)/shard_map/all_to_all | solution.py:248
  19.1 1.9 %collective-permute-start.5 = (bf16[250,4096]{1,0:T(8,128)(2,1)}, bf16[250,4096]{1,0:T(8,128)(2,1)}, u32[]{:S(2)}, u32[]{:S(2)}) collective-permute-start(bf16[250,4096]{1,0:T(8,128)(2,1)} %refs_2_.1), channel_id=1, source_target_pairs={{0,32},{32,0},{1,33},{33,1},{2,34},{34,2},{3,35},{35,3},{4,36},{36... | collective-permute-start | bytes 6144008 | tf_op jit(solution)/shard_map/ppermute | solution.py:252
  21.0 0.0 copy-done
  21.0 2.4 %collective-permute-start.4 = (bf16[250,2048]{1,0:T(8,128)(2,1)S(1)}, bf16[250,2048]{1,0:T(8,128)(2,1)S(1)}, u32[]{:S(2)}, u32[]{:S(2)}) collective-permute-start(bf16[250,2048]{1,0:T(8,128)(2,1)S(1)} %copy-done), channel_id=1, source_target_pairs={{0,32},{32,0},{1,33},{33,1},{2,34},{34,2},{3,35},{35,3},{4,36},{36... | collective-permute-start | bytes 3072008 | tf_op jit(solution)/shard_map/ppermute | solution.py:252
  23.4 19.6 %all-to-all-done = bf16[64,48,128]{2,1,0:T(8,128)(2,1)S(1)} async-done(((bf16[64,48,128]{2,1,0:T(8,128)(2,1)}), bf16[64,48,128]{2,1,0:T(8,128)(2,1)S(1)}, u32[]{:S(2)}, u32[]{:S(2)}) %all-to-all-start) | async-done | bytes 786464 | tf_op jit(solution)/shard_map/all_to_all | solution.py:248
  43.0 1.0 shard_map.68
  44.0 3.4 %collective-permute-start = (bf16[768,256]{1,0:T(8,128)(2,1)S(1)}, bf16[768,256]{1,0:T(8,128)(2,1)S(1)}, u32[]{:S(2)}, u32[]{:S(2)}) collective-permute-start(bf16[768,256]{1,0:T(8,128)(2,1)S(1)} %get-tuple-element.17.refs_4_.refs_0_), channel_id=1, source_target_pairs={{0,1},{1,2},{2,3},{3,0},{4,5},{5,6},{6,7},{7,4},{8,9},{9,10},{10,1... | collective-permute-start | bytes 1179656 | tf_op jit(solution)/shard_map/ppermute | solution.py:256
  47.4 3.7 %collective-permute-start.2 = (bf16[768,256]{1,0:T(8,128)(2,1)}, bf16[768,256]{1,0:T(8,128)(2,1)S(1)}, u32[]{:S(2)}, u32[]{:S(2)}) collective-permute-start(bf16[768,256]{1,0:T(8,128)(2,1)} %get-tuple-element.18.refs_5_.refs_1_), channel_id=1, source_target_pairs={{0,3},{1,0},{2,1},{3,2},{4,7},{5,4},{6,5},{7,6},{8,11},{9,8},{10,9... | collective-permute-start | bytes 1179656 | tf_op jit(solution)/shard_map/ppermute | solution.py:256
  51.1 3.5 %collective-permute-start.6 = (bf16[768,256]{1,0:T(8,128)(2,1)S(1)}, bf16[768,256]{1,0:T(8,128)(2,1)}, u32[]{:S(2)}, u32[]{:S(2)}) collective-permute-start(bf16[768,256]{1,0:T(8,128)(2,1)S(1)} %get-tuple-element.17.refs_4_.refs_0_), channel_id=1, source_target_pairs={{0,3},{1,0},{2,1},{3,2},{4,7},{5,4},{6,5},{7,6},{8,11},{9,8},{10,9... | collective-permute-start | bytes 1179656 | tf_op jit(solution)/shard_map/ppermute | solution.py:256
  54.6 0.0 collective-permute-done.4.refs_1_.s1_ref
  54.6 2.4 %collective-permute-start.7 = (bf16[768,256]{1,0:T(8,128)(2,1)}, bf16[768,256]{1,0:T(8,128)(2,1)}, u32[]{:S(2)}, u32[]{:S(2)}) collective-permute-start(bf16[768,256]{1,0:T(8,128)(2,1)} %get-tuple-element.18.refs_5_.refs_1_), channel_id=1, source_target_pairs={{0,1},{1,2},{2,3},{3,0},{4,5},{5,6},{6,7},{7,4},{8,9},{9,10},{10,1... | collective-permute-start | bytes 1179656 | tf_op jit(solution)/shard_map/ppermute | solution.py:256
  57.0 0.0 collective-permute-done.refs_8_.refs_6_
  57.0 2.2 %collective-permute-start.1 = (bf16[768,256]{1,0:T(8,128)(2,1)S(1)}, bf16[768,256]{1,0:T(8,128)(2,1)}, u32[]{:S(2)}, u32[]{:S(2)}) collective-permute-start(bf16[768,256]{1,0:T(8,128)(2,1)S(1)} %collective-permute-done.refs_8_.refs_6_), channel_id=1, source_target_pairs={{0,1},{1,2},{2,3},{3,0},{4,5},{5,6},{6,7},{7,4},{8,9},{9,10},{10,1... | collective-permute-start | bytes 1179656 | tf_op jit(solution)/shard_map/ppermute | solution.py:256
  59.2 2.4 %collective-permute-done.2.refs_7_.refs_3_ = bf16[768,256]{1,0:T(8,128)(2,1)S(1)} collective-permute-done((bf16[768,256]{1,0:T(8,128)(2,1)}, bf16[768,256]{1,0:T(8,128)(2,1)S(1)}, u32[]{:S(2)}, u32[]{:S(2)}) %collective-permute-start.2) | collective-permute-done | bytes 393248 | tf_op jit(solution)/shard_map/ppermute | solution.py:256
  61.6 4.9 %collective-permute-start.3 = (bf16[768,256]{1,0:T(8,128)(2,1)S(1)}, bf16[768,256]{1,0:T(8,128)(2,1)}, u32[]{:S(2)}, u32[]{:S(2)}) collective-permute-start(bf16[768,256]{1,0:T(8,128)(2,1)S(1)} %collective-permute-done.2.refs_7_.refs_3_), channel_id=1, source_target_pairs={{0,3},{1,0},{2,1},{3,2},{4,7},{5,4},{6,5},{7,6},{8,11},{9,8},{10,9... | collective-permute-start | bytes 1179656 | tf_op jit(solution)/shard_map/ppermute | solution.py:256
  66.4 3.7 %collective-permute-done.6.refs_6_.refs_2_ = bf16[768,256]{1,0:T(8,128)(2,1)} collective-permute-done((bf16[768,256]{1,0:T(8,128)(2,1)S(1)}, bf16[768,256]{1,0:T(8,128)(2,1)}, u32[]{:S(2)}, u32[]{:S(2)}) %collective-permute-start.6) | collective-permute-done | bytes 393248 | tf_op jit(solution)/shard_map/ppermute | solution.py:256
  70.1 0.0 collective-permute-done.7.refs_9_.refs_7_
  70.1 0.0 collective-permute-done.5.refs_3_
  70.1 0.0 copy-start.1
  70.1 1.6 %copy-done.1 = bf16[250,4096]{1,0:T(8,128)(2,1)S(1)} copy-done((bf16[250,4096]{1,0:T(8,128)(2,1)S(1)}, bf16[250,4096]{1,0:T(8,128)(2,1)}, u32[]{:S(2)}) %copy-start.1) | copy-done | bytes 2048024
  71.7 6.4 %shard_map.69 = (f32[2,250,256]{2,1,0:T(8,128)S(1)}, f32[2,250,256]{2,1,0:T(8,128)S(1)}, bf16[2,250,1024]{2,1,0:T(8,128)(2,1)S(1)}, bf16[2,250,1024]{2,1,0:T(8,128)(2,1)S(1)}) custom-call(s32[1]{0:T(128)} %bitcast.x_ref, bf16[250,2048]{1,0:T(8,128)(2,1)S(1)} %copy-done, bf16[250,2048]{1,0:T(8,128)(2,1)S(1)} %collective-permute-done.4.refs_1_.s1_ref, ...), custom_call_target="tpu_custom_call" | custom-call | tf_op jit(solution)/shard_map/pallas_call | solution.py:34
  78.1 0.0 collective-permute-done.1.lo_ref.refs_4_
  78.1 0.0 collective-permute-done.3.hi_ref.refs_5_
  78.1 2.1 %shard_map.70 = (f32[2,250,256]{2,1,0:T(8,128)S(1)}, f32[2,250,256]{2,1,0:T(8,128)S(1)}, f32[32,8,256]{2,1,0:T(8,128)S(1)}) custom-call(s32[1]{0:T(128)} %bitcast.x_ref, bf16[768,256]{1,0:T(8,128)(2,1)} %collective-permute-done.1.lo_ref.refs_4_, bf16[768,256]{1,0:T(8,128)(2,1)} %collective-permute-done.3.hi_ref.refs_5_, ...), custom_call_target="tpu_custom_call" | custom-call | flops 524288000 | bytes 5144580 | tf_op jit(solution)/shard_map/pallas_call | solution.py:34
  80.3 18.4 %all_to_all.25.p_ref = f32[32,8,256]{2,1,0:T(8,128)S(1)} all-to-all(f32[32,8,256]{2,1,0:T(8,128)S(1)} %get-tuple-element.23), channel_id=1, replica_groups=mesh['z'=8,'core'=2,'yq'=4,'yp'=2,'x'=4] {'yq','yp','x'}, dimensions={0} | all-to-all | bytes 524288 | tf_op jit(solution)/shard_map/all_to_all | solution.py:248
  98.7 0.1 shard_map.71
  98.8 10.8 %all_to_all.26.p_ref = f32[8,8,256]{2,1,0:T(8,128)S(1)} all-to-all(f32[8,8,256]{2,1,0:T(8,128)S(1)} %shard_map.71), channel_id=1, replica_groups=mesh['z'=8,'core'=2,'yq'=4,'yp'=2,'x'=4] {'z'}, dimensions={0} | all-to-all | bytes 131072 | tf_op jit(solution)/shard_map/all_to_all | solution.py:248
  109.5 0.9 shard_map.72
  110.5 0.0 copy-start.2
  110.5 1.0 copy-done.2
  111.4 4.5 %all-to-all-start.3 = ((bf16[8,256,256]{2,1,0:T(8,128)(2,1)}), bf16[8,256,256]{2,1,0:T(8,128)(2,1)S(1)}, u32[]{:S(2)}, u32[]{:S(2)}) async-start(bf16[8,256,256]{2,1,0:T(8,128)(2,1)} %copy-done.2), calls=%async_computation.3 | async-start | bytes 2097152 | tf_op jit(solution)/shard_map/all_to_all | solution.py:248
  115.9 1.4 shard_map.73.full_s
  117.3 0.5 shard_map.74._
  117.8 1.9 %collective-permute-start.8 = (bf16[250,2176]{1,0:T(8,128)(2,1)S(1)}, bf16[250,2176]{1,0:T(8,128)(2,1)}, u32[]{:S(2)}, u32[]{:S(2)}) collective-permute-start(bf16[250,2176]{1,0:T(8,128)(2,1)S(1)} %shard_map.74._), channel_id=1, source_target_pairs={{0,32},{32,0},{1,33},{33,1},{2,34},{34,2},{3,35},{35,3},{4,36},{36... | collective-permute-start | bytes 3264008 | tf_op jit(solution)/shard_map/ppermute | solution.py:252
  119.7 6.2 %all-to-all-done.3.r_ref = bf16[8,256,256]{2,1,0:T(8,128)(2,1)S(1)} async-done(((bf16[8,256,256]{2,1,0:T(8,128)(2,1)}), bf16[8,256,256]{2,1,0:T(8,128)(2,1)S(1)}, u32[]{:S(2)}, u32[]{:S(2)}) %all-to-all-start.3) | async-done | bytes 1048608 | tf_op jit(solution)/shard_map/all_to_all | solution.py:248
  126.0 0.2 shard_map.76
  126.2 0.0 copy-start.3
  126.2 0.6 copy-done.3
  126.8 3.8 %all-to-all-start.4 = ((bf16[32,16,128]{2,1,0:T(8,128)(2,1)}), bf16[32,16,128]{2,1,0:T(8,128)(2,1)S(1)}, u32[]{:S(2)}, u32[]{:S(2)}) async-start(bf16[32,16,128]{2,1,0:T(8,128)(2,1)} %copy-done.3), calls=%async_computation.4 | async-start | bytes 262144 | tf_op jit(solution)/shard_map/all_to_all | solution.py:248
  130.7 0.0 collective-permute-done.8.arrived
  130.7 2.7 %shard_map.75 = (bf16[250,2048]{1,0:T(8,128)(2,1)}, f32[1,1]{1,0:T(1,128)}) custom-call(bf16[2,250,256]{2,1,0:T(8,128)(2,1)S(1)} %get-tuple-element.26.g_ref, bf16[2048,256]{1,0:T(8,128)(2,1)S(1)} %shard_map.73.full_s, f32[8,128]{1,0:T(8,128)S(1)} %get-tuple-element.27.refs_8_.kl_ref, bf16[250,2176]{1,0:T(8,128)(2,1)} %collective-permute-done.8.arrived), custom_call_target="tpu_custom_call" | custom-call | flops 262144000 | bytes 3420676 | tf_op jit(solution)/shard_map/pallas_call | solution.py:34
  133.4 9.7 %all-to-all-done.4.r_ref = bf16[32,16,128]{2,1,0:T(8,128)(2,1)S(1)} async-done(((bf16[32,16,128]{2,1,0:T(8,128)(2,1)}), bf16[32,16,128]{2,1,0:T(8,128)(2,1)S(1)}, u32[]{:S(2)}, u32[]{:S(2)}) %all-to-all-start.4) | async-done | bytes 131104 | tf_op jit(solution)/shard_map/all_to_all | solution.py:248
  143.0 0.7 shard_map.77
Async XLA Ops:
  0.6 20.4 %copy-start = (bf16[250,2048]{1,0:T(8,128)(2,1)S(1)}, bf16[250,2048]{1,0:T(8,128)(2,1)}, u32[]{:S(2)}) copy-start(bf16[250,2048]{1,0:T(8,128)(2,1)} %s0_ref.1) | copy-start | bytes 3072004
  2.5 40.6 %all-to-all-start = ((bf16[64,48,128]{2,1,0:T(8,128)(2,1)}), bf16[64,48,128]{2,1,0:T(8,128)(2,1)S(1)}, u32[]{:S(2)}, u32[]{:S(2)}) async-start(bf16[64,48,128]{2,1,0:T(8,128)(2,1)} %shard_map.67), calls=%async_computation | async-start | bytes 1572864 | tf_op jit(solution)/shard_map/all_to_all | solution.py:248
  19.1 51.1 %collective-permute-start.5 = (bf16[250,4096]{1,0:T(8,128)(2,1)}, bf16[250,4096]{1,0:T(8,128)(2,1)}, u32[]{:S(2)}, u32[]{:S(2)}) collective-permute-start(bf16[250,4096]{1,0:T(8,128)(2,1)} %refs_2_.1), channel_id=1, source_target_pairs={{0,32},{32,0},{1,33},{33,1},{2,34},{34,2},{3,35},{35,3},{4,36},{36... | collective-permute-start | bytes 6144008 | tf_op jit(solution)/shard_map/ppermute | solution.py:252
  21.0 33.6 %collective-permute-start.4 = (bf16[250,2048]{1,0:T(8,128)(2,1)S(1)}, bf16[250,2048]{1,0:T(8,128)(2,1)S(1)}, u32[]{:S(2)}, u32[]{:S(2)}) collective-permute-start(bf16[250,2048]{1,0:T(8,128)(2,1)S(1)} %copy-done), channel_id=1, source_target_pairs={{0,32},{32,0},{1,33},{33,1},{2,34},{34,2},{3,35},{35,3},{4,36},{36... | collective-permute-start | bytes 3072008 | tf_op jit(solution)/shard_map/ppermute | solution.py:252
  44.0 12.9 %collective-permute-start = (bf16[768,256]{1,0:T(8,128)(2,1)S(1)}, bf16[768,256]{1,0:T(8,128)(2,1)S(1)}, u32[]{:S(2)}, u32[]{:S(2)}) collective-permute-start(bf16[768,256]{1,0:T(8,128)(2,1)S(1)} %get-tuple-element.17.refs_4_.refs_0_), channel_id=1, source_target_pairs={{0,1},{1,2},{2,3},{3,0},{4,5},{5,6},{6,7},{7,4},{8,9},{9,10},{10,1... | collective-permute-start | bytes 1179656 | tf_op jit(solution)/shard_map/ppermute | solution.py:256
  47.4 14.2 %collective-permute-start.2 = (bf16[768,256]{1,0:T(8,128)(2,1)}, bf16[768,256]{1,0:T(8,128)(2,1)S(1)}, u32[]{:S(2)}, u32[]{:S(2)}) collective-permute-start(bf16[768,256]{1,0:T(8,128)(2,1)} %get-tuple-element.18.refs_5_.refs_1_), channel_id=1, source_target_pairs={{0,3},{1,0},{2,1},{3,2},{4,7},{5,4},{6,5},{7,6},{8,11},{9,8},{10,9... | collective-permute-start | bytes 1179656 | tf_op jit(solution)/shard_map/ppermute | solution.py:256
  51.1 19.0 %collective-permute-start.6 = (bf16[768,256]{1,0:T(8,128)(2,1)S(1)}, bf16[768,256]{1,0:T(8,128)(2,1)}, u32[]{:S(2)}, u32[]{:S(2)}) collective-permute-start(bf16[768,256]{1,0:T(8,128)(2,1)S(1)} %get-tuple-element.17.refs_4_.refs_0_), channel_id=1, source_target_pairs={{0,3},{1,0},{2,1},{3,2},{4,7},{5,4},{6,5},{7,6},{8,11},{9,8},{10,9... | collective-permute-start | bytes 1179656 | tf_op jit(solution)/shard_map/ppermute | solution.py:256
  54.6 15.6 %collective-permute-start.7 = (bf16[768,256]{1,0:T(8,128)(2,1)}, bf16[768,256]{1,0:T(8,128)(2,1)}, u32[]{:S(2)}, u32[]{:S(2)}) collective-permute-start(bf16[768,256]{1,0:T(8,128)(2,1)} %get-tuple-element.18.refs_5_.refs_1_), channel_id=1, source_target_pairs={{0,1},{1,2},{2,3},{3,0},{4,5},{5,6},{6,7},{7,4},{8,9},{9,10},{10,1... | collective-permute-start | bytes 1179656 | tf_op jit(solution)/shard_map/ppermute | solution.py:256
  57.0 21.1 %collective-permute-start.1 = (bf16[768,256]{1,0:T(8,128)(2,1)S(1)}, bf16[768,256]{1,0:T(8,128)(2,1)}, u32[]{:S(2)}, u32[]{:S(2)}) collective-permute-start(bf16[768,256]{1,0:T(8,128)(2,1)S(1)} %collective-permute-done.refs_8_.refs_6_), channel_id=1, source_target_pairs={{0,1},{1,2},{2,3},{3,0},{4,5},{5,6},{6,7},{7,4},{8,9},{9,10},{10,1... | collective-permute-start | bytes 1179656 | tf_op jit(solution)/shard_map/ppermute | solution.py:256
  61.6 16.5 %collective-permute-start.3 = (bf16[768,256]{1,0:T(8,128)(2,1)S(1)}, bf16[768,256]{1,0:T(8,128)(2,1)}, u32[]{:S(2)}, u32[]{:S(2)}) collective-permute-start(bf16[768,256]{1,0:T(8,128)(2,1)S(1)} %collective-permute-done.2.refs_7_.refs_3_), channel_id=1, source_target_pairs={{0,3},{1,0},{2,1},{3,2},{4,7},{5,4},{6,5},{7,6},{8,11},{9,8},{10,9... | collective-permute-start | bytes 1179656 | tf_op jit(solution)/shard_map/ppermute | solution.py:256
  70.1 1.6 %copy-start.1 = (bf16[250,4096]{1,0:T(8,128)(2,1)S(1)}, bf16[250,4096]{1,0:T(8,128)(2,1)}, u32[]{:S(2)}) copy-start(bf16[250,4096]{1,0:T(8,128)(2,1)} %refs_2_.1) | copy-start | bytes 6144004
  110.5 1.0 copy-start.2
  111.4 14.5 %all-to-all-start.3 = ((bf16[8,256,256]{2,1,0:T(8,128)(2,1)}), bf16[8,256,256]{2,1,0:T(8,128)(2,1)S(1)}, u32[]{:S(2)}, u32[]{:S(2)}) async-start(bf16[8,256,256]{2,1,0:T(8,128)(2,1)} %copy-done.2), calls=%async_computation.3 | async-start | bytes 2097152 | tf_op jit(solution)/shard_map/all_to_all | solution.py:248
  117.8 12.9 %collective-permute-start.8 = (bf16[250,2176]{1,0:T(8,128)(2,1)S(1)}, bf16[250,2176]{1,0:T(8,128)(2,1)}, u32[]{:S(2)}, u32[]{:S(2)}) collective-permute-start(bf16[250,2176]{1,0:T(8,128)(2,1)S(1)} %shard_map.74._), channel_id=1, source_target_pairs={{0,32},{32,0},{1,33},{33,1},{2,34},{34,2},{3,35},{35,3},{4,36},{36... | collective-permute-start | bytes 3264008 | tf_op jit(solution)/shard_map/ppermute | solution.py:252
  126.2 0.6 copy-start.3
  126.8 16.2 %all-to-all-start.4 = ((bf16[32,16,128]{2,1,0:T(8,128)(2,1)}), bf16[32,16,128]{2,1,0:T(8,128)(2,1)S(1)}, u32[]{:S(2)}, u32[]{:S(2)}) async-start(bf16[32,16,128]{2,1,0:T(8,128)(2,1)} %copy-done.3), calls=%async_computation.4 | async-start | bytes 262144 | tf_op jit(solution)/shard_map/all_to_all | solution.py:248

commit v4 on v3

--- a/solution.py
+++ b/solution.py
@@ -80,20 +80,24 @@
 
 def merged(parts):
     n = parts.shape[0]
-    m = parts[0, 0:2]
+    m = parts[0, 0:4]
     for i in range(1, n):
-        m = jnp.maximum(m, parts[i, 0:2])
+        m = jnp.maximum(m, parts[i, 0:4])
     total = jnp.zeros_like(m)
-    cross = jnp.zeros((1, m.shape[1]), F32)
+    cross = jnp.zeros((2, m.shape[1]), F32)
     for i in range(n):
-        w = jnp.exp(parts[i, 0:2] - m)
-        total = total + w * parts[i, 2:4]
-        cross = cross + w[0:1] * parts[i, 4:5]
-    return m, total, cross
-
-
-def rows_of(m, total, cross):
-    return jnp.concatenate([m, total, cross, jnp.zeros((3, m.shape[1]), F32)], axis=0)
+        w = jnp.exp(parts[i, 0:4] - m)
+        total = total + w
+        cross = cross + w[0:2] * parts[i, 4:6]
+    return m + jnp.log(total), cross / total[0:2]
+
+
+def rows_of(lse, cross):
+    return jnp.concatenate([lse, cross, jnp.zeros((2, lse.shape[1]), F32)], axis=0)
+
+
+def halves(v):
+    return [v[:, 0:SIDE], v[:, SIDE:ALL]]
 
 
 def early_kernel(x_ref, *refs):
@@ -159,7 +163,8 @@
         et = jnp.exp(lt - mt)
         new = (et, jnp.exp(ls - ms), et * (lt - ls))
         sums = [a + jnp.sum(v, axis=0, keepdims=True) for a, v in zip(sums, new)]
-    stat = jnp.concatenate([mt, ms] + sums + [jnp.zeros((3, ALL), F32)], axis=0)
+    lse = halves(mt + jnp.log(sums[0])) + halves(ms + jnp.log(sums[1]))
+    stat = rows_of(jnp.concatenate(lse, axis=0), jnp.concatenate(halves(sums[2] / sums[0]), axis=0))
     for i in range(Y * X):
         stat_ref[i] = stat
 
@@ -183,10 +188,10 @@
 
 
 def grads_kernel(p_ref, ls_ref, lt_ref, s0_ref, s1_ref, g_ref, by_ypx_ref, kl_ref, terms):
-    m, total, cross = merged(p_ref)
-    lse = m + jnp.log(total)
-    lse_t, lse_s = lse[0:1], lse[1:2]
-    kl = cross / total[0:1] - lse_t + lse_s
+    lse, cross = merged(p_ref)
+    lse_t = jnp.concatenate([lse[0:1], lse[1:2]], axis=1)
+    lse_s = jnp.concatenate([lse[2:3], lse[3:4]], axis=1)
+    kl = jnp.concatenate([cross[0:1], cross[1:2]], axis=1) - lse_t + lse_s
     lane = lax.broadcasted_iota(jnp.int32, (1, ALL), 1)
     padding = (lane >= SIDE) & ((lane & (HALF - 1)) >= TOK - HALF)
     kl_ref[...] = jnp.broadcast_to(jnp.sum(jnp.where(padding, 0.0, kl), axis=1, keepdims=True), kl_ref.shape)
@@ -307,7 +312,7 @@
     )
     ls, lt, stat = call(
         late_kernel,
-        (logit, logit, array((Y * X, 8, ALL), F32)),
+        (logit, logit, array((Y * X, 8, SIDE), F32)),
         xi,
         *far,
         far_s,
@@ -319,7 +324,7 @@
         flops=8 * rows * ALL * Y * FT,
     )
     stat = exchange(stat, ("yq", "yp", "x"))
-    stat = call(merge_kernel, array((Z, 8, ALL), F32), stat)
+    stat = call(merge_kernel, array((Z, 8, SIDE), F32), stat)
     stat = exchange(stat, "z")
     grads, by_ypx, kl = call(
         grads_kernel,

time: 145 us -> 143 us (0.986)
  blocking collectives: 29.2 us -> 27.6 us
    all_to_all x2, blocking collectives: 29.2 us -> 27.6 us  [exchange(): return lax.all_to_all(v, axes, 0, 0, tiled=True)]
  transfers between devices with their start and end apart: 12 -> 12, of which waited for: 5 -> 5; matrix products, arithmetic and copies ran while one was open for 0% -> 0% of each run, Pallas kernels for 8% -> 9%
where the time goes in v4:
time: 143 us; the launch traced here: 142 us
  starting transfers between devices  51.3 us (36%)
  waiting for transfers between devices  41.6 us (29%)
  blocking collectives  27.6 us (19%)
  Pallas kernels  17.8 us (12%)
  local copies, waits for them, and re-layouts  3.2 us (2%)
    all_to_all x3, waiting for transfers between devices, exchange(): return lax.all_to_all(v, axes, 0, 0, tiled=True)  35.5 us
    all_to_all x2, blocking collectives, exchange(): return lax.all_to_all(v, axes, 0, 0, tiled=True)  27.6 us
    all_to_all x3, starting transfers between devices, exchange(): return lax.all_to_all(v, axes, 0, 0, tiled=True)  25.1 us
    ppermute x6, starting transfers between devices, along_x(): return lax.ppermute(v, 'x', [(i, (i + step) % X) for i in range(X)])  19.9 us
    pallas_call x11, Pallas kernels, call(): pl.pallas_call(kernel, out_shape=out, in_specs=specs, out_specs=outs, scr...  17.8 us
    ppermute x3, starting transfers between devices, swap(): return lax.ppermute(v, 'core', [(0, 1), (1, 0)])  6.25 us
    ppermute x6, waiting for transfers between devices, along_x(): return lax.ppermute(v, 'x', [(i, (i + step) % X) for i in range(X)])  6.09 us
    unnamed x8, local copies, waits for them, and re-layouts  3.2 us
  transfers between devices with their start and end apart: 12, of which 5 were waited for; matrix products, arithmetic and copies ran while one was open for 0% of the time, Pallas kernels for 9%

profile of v4, /device:TPU:8, one launch (start us, length us, event | category | flops | bytes accessed | tf_op | source)
XLA Modules:
  0.0 142.3 jit_solution(6339809286190442505)
XLA Ops:
  0.6 0.0 copy-start
  0.6 1.8 %shard_map.67 = bf16[64,48,128]{2,1,0:T(8,128)(2,1)} custom-call(bf16[30,64]{1,0:T(8,128)(2,1)} %s_any.1, bf16[30,128]{1,0:T(8,128)(2,1)} %t_any.1), custom_call_target="tpu_custom_call" | custom-call | bytes 797952 | tf_op jit(solution)/shard_map/pallas_call | solution.py:34
  2.5 16.6 %all-to-all-start = ((bf16[64,48,128]{2,1,0:T(8,128)(2,1)}), bf16[64,48,128]{2,1,0:T(8,128)(2,1)S(1)}, u32[]{:S(2)}, u32[]{:S(2)}) async-start(bf16[64,48,128]{2,1,0:T(8,128)(2,1)} %shard_map.67), calls=%async_computation | async-start | bytes 1572864 | tf_op jit(solution)/shard_map/all_to_all | solution.py:253
  19.1 1.9 %collective-permute-start.5 = (bf16[250,4096]{1,0:T(8,128)(2,1)}, bf16[250,4096]{1,0:T(8,128)(2,1)}, u32[]{:S(2)}, u32[]{:S(2)}) collective-permute-start(bf16[250,4096]{1,0:T(8,128)(2,1)} %refs_2_.1), channel_id=1, source_target_pairs={{0,32},{32,0},{1,33},{33,1},{2,34},{34,2},{3,35},{35,3},{4,36},{36... | collective-permute-start | bytes 6144008 | tf_op jit(solution)/shard_map/ppermute | solution.py:257
  21.0 0.0 copy-done
  21.0 2.4 %collective-permute-start.4 = (bf16[250,2048]{1,0:T(8,128)(2,1)S(1)}, bf16[250,2048]{1,0:T(8,128)(2,1)S(1)}, u32[]{:S(2)}, u32[]{:S(2)}) collective-permute-start(bf16[250,2048]{1,0:T(8,128)(2,1)S(1)} %copy-done), channel_id=1, source_target_pairs={{0,32},{32,0},{1,33},{33,1},{2,34},{34,2},{3,35},{35,3},{4,36},{36... | collective-permute-start | bytes 3072008 | tf_op jit(solution)/shard_map/ppermute | solution.py:257
  23.4 19.6 %all-to-all-done = bf16[64,48,128]{2,1,0:T(8,128)(2,1)S(1)} async-done(((bf16[64,48,128]{2,1,0:T(8,128)(2,1)}), bf16[64,48,128]{2,1,0:T(8,128)(2,1)S(1)}, u32[]{:S(2)}, u32[]{:S(2)}) %all-to-all-start) | async-done | bytes 786464 | tf_op jit(solution)/shard_map/all_to_all | solution.py:253
  43.0 1.0 shard_map.68
  44.0 3.4 %collective-permute-start = (bf16[768,256]{1,0:T(8,128)(2,1)S(1)}, bf16[768,256]{1,0:T(8,128)(2,1)S(1)}, u32[]{:S(2)}, u32[]{:S(2)}) collective-permute-start(bf16[768,256]{1,0:T(8,128)(2,1)S(1)} %get-tuple-element.17.refs_4_.refs_0_), channel_id=1, source_target_pairs={{0,1},{1,2},{2,3},{3,0},{4,5},{5,6},{6,7},{7,4},{8,9},{9,10},{10,1... | collective-permute-start | bytes 1179656 | tf_op jit(solution)/shard_map/ppermute | solution.py:261
  47.4 3.7 %collective-permute-start.2 = (bf16[768,256]{1,0:T(8,128)(2,1)}, bf16[768,256]{1,0:T(8,128)(2,1)S(1)}, u32[]{:S(2)}, u32[]{:S(2)}) collective-permute-start(bf16[768,256]{1,0:T(8,128)(2,1)} %get-tuple-element.18.refs_5_.refs_1_), channel_id=1, source_target_pairs={{0,3},{1,0},{2,1},{3,2},{4,7},{5,4},{6,5},{7,6},{8,11},{9,8},{10,9... | collective-permute-start | bytes 1179656 | tf_op jit(solution)/shard_map/ppermute | solution.py:261
  51.1 3.5 %collective-permute-start.6 = (bf16[768,256]{1,0:T(8,128)(2,1)S(1)}, bf16[768,256]{1,0:T(8,128)(2,1)}, u32[]{:S(2)}, u32[]{:S(2)}) collective-permute-start(bf16[768,256]{1,0:T(8,128)(2,1)S(1)} %get-tuple-element.17.refs_4_.refs_0_), channel_id=1, source_target_pairs={{0,3},{1,0},{2,1},{3,2},{4,7},{5,4},{6,5},{7,6},{8,11},{9,8},{10,9... | collective-permute-start | bytes 1179656 | tf_op jit(solution)/shard_map/ppermute | solution.py:261
  54.6 0.0 collective-permute-done.4.refs_1_.s1_ref
  54.6 2.4 %collective-permute-start.7 = (bf16[768,256]{1,0:T(8,128)(2,1)}, bf16[768,256]{1,0:T(8,128)(2,1)}, u32[]{:S(2)}, u32[]{:S(2)}) collective-permute-start(bf16[768,256]{1,0:T(8,128)(2,1)} %get-tuple-element.18.refs_5_.refs_1_), channel_id=1, source_target_pairs={{0,1},{1,2},{2,3},{3,0},{4,5},{5,6},{6,7},{7,4},{8,9},{9,10},{10,1... | collective-permute-start | bytes 1179656 | tf_op jit(solution)/shard_map/ppermute | solution.py:261
  57.0 0.0 collective-permute-done.refs_8_.refs_6_
  57.0 2.2 %collective-permute-start.1 = (bf16[768,256]{1,0:T(8,128)(2,1)S(1)}, bf16[768,256]{1,0:T(8,128)(2,1)}, u32[]{:S(2)}, u32[]{:S(2)}) collective-permute-start(bf16[768,256]{1,0:T(8,128)(2,1)S(1)} %collective-permute-done.refs_8_.refs_6_), channel_id=1, source_target_pairs={{0,1},{1,2},{2,3},{3,0},{4,5},{5,6},{6,7},{7,4},{8,9},{9,10},{10,1... | collective-permute-start | bytes 1179656 | tf_op jit(solution)/shard_map/ppermute | solution.py:261
  59.2 2.4 %collective-permute-done.2.refs_7_.refs_3_ = bf16[768,256]{1,0:T(8,128)(2,1)S(1)} collective-permute-done((bf16[768,256]{1,0:T(8,128)(2,1)}, bf16[768,256]{1,0:T(8,128)(2,1)S(1)}, u32[]{:S(2)}, u32[]{:S(2)}) %collective-permute-start.2) | collective-permute-done | bytes 393248 | tf_op jit(solution)/shard_map/ppermute | solution.py:261
  61.6 4.9 %collective-permute-start.3 = (bf16[768,256]{1,0:T(8,128)(2,1)S(1)}, bf16[768,256]{1,0:T(8,128)(2,1)}, u32[]{:S(2)}, u32[]{:S(2)}) collective-permute-start(bf16[768,256]{1,0:T(8,128)(2,1)S(1)} %collective-permute-done.2.refs_7_.refs_3_), channel_id=1, source_target_pairs={{0,3},{1,0},{2,1},{3,2},{4,7},{5,4},{6,5},{7,6},{8,11},{9,8},{10,9... | collective-permute-start | bytes 1179656 | tf_op jit(solution)/shard_map/ppermute | solution.py:261
  66.4 3.7 %collective-permute-done.6.refs_6_.refs_2_ = bf16[768,256]{1,0:T(8,128)(2,1)} collective-permute-done((bf16[768,256]{1,0:T(8,128)(2,1)S(1)}, bf16[768,256]{1,0:T(8,128)(2,1)}, u32[]{:S(2)}, u32[]{:S(2)}) %collective-permute-start.6) | collective-permute-done | bytes 393248 | tf_op jit(solution)/shard_map/ppermute | solution.py:261
  70.1 0.0 collective-permute-done.7.refs_9_.refs_7_
  70.1 0.0 collective-permute-done.5.refs_3_
  70.1 0.0 copy-start.1
  70.1 1.6 %copy-done.1 = bf16[250,4096]{1,0:T(8,128)(2,1)S(1)} copy-done((bf16[250,4096]{1,0:T(8,128)(2,1)S(1)}, bf16[250,4096]{1,0:T(8,128)(2,1)}, u32[]{:S(2)}) %copy-start.1) | copy-done | bytes 2048024
  71.7 6.4 %shard_map.69 = (f32[2,250,256]{2,1,0:T(8,128)S(1)}, f32[2,250,256]{2,1,0:T(8,128)S(1)}, bf16[2,250,1024]{2,1,0:T(8,128)(2,1)S(1)}, bf16[2,250,1024]{2,1,0:T(8,128)(2,1)S(1)}) custom-call(s32[1]{0:T(128)} %bitcast.x_ref, bf16[250,2048]{1,0:T(8,128)(2,1)S(1)} %copy-done, bf16[250,2048]{1,0:T(8,128)(2,1)S(1)} %collective-permute-done.4.refs_1_.s1_ref, ...), custom_call_target="tpu_custom_call" | custom-call | tf_op jit(solution)/shard_map/pallas_call | solution.py:34
  78.1 0.0 collective-permute-done.1.lo_ref.refs_4_
  78.1 0.0 collective-permute-done.3.hi_ref.refs_5_
  78.1 2.2 %shard_map.70 = (f32[2,250,256]{2,1,0:T(8,128)S(1)}, f32[2,250,256]{2,1,0:T(8,128)S(1)}, f32[32,8,128]{2,1,0:T(8,128)S(1)}) custom-call(s32[1]{0:T(128)} %bitcast.x_ref, bf16[768,256]{1,0:T(8,128)(2,1)} %collective-permute-done.1.lo_ref.refs_4_, bf16[768,256]{1,0:T(8,128)(2,1)} %collective-permute-done.3.hi_ref.refs_5_, ...), custom_call_target="tpu_custom_call" | custom-call | flops 524288000 | bytes 5013508 | tf_op jit(solution)/shard_map/pallas_call | solution.py:34
  80.3 17.2 %all_to_all.25.p_ref = f32[32,8,128]{2,1,0:T(8,128)S(1)} all-to-all(f32[32,8,128]{2,1,0:T(8,128)S(1)} %get-tuple-element.23), channel_id=1, replica_groups=mesh['z'=8,'core'=2,'yq'=4,'yp'=2,'x'=4] {'yq','yp','x'}, dimensions={0} | all-to-all | bytes 262144 | tf_op jit(solution)/shard_map/all_to_all | solution.py:253
  97.4 0.1 shard_map.71
  97.5 10.4 %all_to_all.26.p_ref = f32[8,8,128]{2,1,0:T(8,128)S(1)} all-to-all(f32[8,8,128]{2,1,0:T(8,128)S(1)} %shard_map.71), channel_id=1, replica_groups=mesh['z'=8,'core'=2,'yq'=4,'yp'=2,'x'=4] {'z'}, dimensions={0} | all-to-all | bytes 65536 | tf_op jit(solution)/shard_map/all_to_all | solution.py:253
  107.9 0.9 shard_map.72
  108.8 0.0 copy-start.2
  108.8 1.0 copy-done.2
  109.8 4.7 %all-to-all-start.3 = ((bf16[8,256,256]{2,1,0:T(8,128)(2,1)}), bf16[8,256,256]{2,1,0:T(8,128)(2,1)S(1)}, u32[]{:S(2)}, u32[]{:S(2)}) async-start(bf16[8,256,256]{2,1,0:T(8,128)(2,1)} %copy-done.2), calls=%async_computation.3 | async-start | bytes 2097152 | tf_op jit(solution)/shard_map/all_to_all | solution.py:253
  114.5 1.4 shard_map.73.full_s
  115.9 0.5 shard_map.74._
  116.4 1.9 %collective-permute-start.8 = (bf16[250,2176]{1,0:T(8,128)(2,1)S(1)}, bf16[250,2176]{1,0:T(8,128)(2,1)}, u32[]{:S(2)}, u32[]{:S(2)}) collective-permute-start(bf16[250,2176]{1,0:T(8,128)(2,1)S(1)} %shard_map.74._), channel_id=1, source_target_pairs={{0,32},{32,0},{1,33},{33,1},{2,34},{34,2},{3,35},{35,3},{4,36},{36... | collective-permute-start | bytes 3264008 | tf_op jit(solution)/shard_map/ppermute | solution.py:257
  118.3 6.2 %all-to-all-done.3.r_ref = bf16[8,256,256]{2,1,0:T(8,128)(2,1)S(1)} async-done(((bf16[8,256,256]{2,1,0:T(8,128)(2,1)}), bf16[8,256,256]{2,1,0:T(8,128)(2,1)S(1)}, u32[]{:S(2)}, u32[]{:S(2)}) %all-to-all-start.3) | async-done | bytes 1048608 | tf_op jit(solution)/shard_map/all_to_all | solution.py:253
  124.5 0.2 shard_map.76
  124.7 0.0 copy-start.3
  124.7 0.6 copy-done.3
  125.4 3.8 %all-to-all-start.4 = ((bf16[32,16,128]{2,1,0:T(8,128)(2,1)}), bf16[32,16,128]{2,1,0:T(8,128)(2,1)S(1)}, u32[]{:S(2)}, u32[]{:S(2)}) async-start(bf16[32,16,128]{2,1,0:T(8,128)(2,1)} %copy-done.3), calls=%async_computation.4 | async-start | bytes 262144 | tf_op jit(solution)/shard_map/all_to_all | solution.py:253
  129.2 0.0 collective-permute-done.8.arrived
  129.2 2.7 %shard_map.75 = (bf16[250,2048]{1,0:T(8,128)(2,1)}, f32[1,1]{1,0:T(1,128)}) custom-call(bf16[2,250,256]{2,1,0:T(8,128)(2,1)S(1)} %get-tuple-element.26.g_ref, bf16[2048,256]{1,0:T(8,128)(2,1)S(1)} %shard_map.73.full_s, f32[8,128]{1,0:T(8,128)S(1)} %get-tuple-element.27.refs_8_.kl_ref, bf16[250,2176]{1,0:T(8,128)(2,1)} %collective-permute-done.8.arrived), custom_call_target="tpu_custom_call" | custom-call | flops 262144000 | bytes 3420676 | tf_op jit(solution)/shard_map/pallas_call | solution.py:34
  131.9 9.7 %all-to-all-done.4.r_ref = bf16[32,16,128]{2,1,0:T(8,128)(2,1)S(1)} async-done(((bf16[32,16,128]{2,1,0:T(8,128)(2,1)}), bf16[32,16,128]{2,1,0:T(8,128)(2,1)S(1)}, u32[]{:S(2)}, u32[]{:S(2)}) %all-to-all-start.4) | async-done | bytes 131104 | tf_op jit(solution)/shard_map/all_to_all | solution.py:253
  141.6 0.7 shard_map.77
Async XLA Ops:
  0.6 20.4 %copy-start = (bf16[250,2048]{1,0:T(8,128)(2,1)S(1)}, bf16[250,2048]{1,0:T(8,128)(2,1)}, u32[]{:S(2)}) copy-start(bf16[250,2048]{1,0:T(8,128)(2,1)} %s0_ref.1) | copy-start | bytes 3072004
  2.5 40.6 %all-to-all-start = ((bf16[64,48,128]{2,1,0:T(8,128)(2,1)}), bf16[64,48,128]{2,1,0:T(8,128)(2,1)S(1)}, u32[]{:S(2)}, u32[]{:S(2)}) async-start(bf16[64,48,128]{2,1,0:T(8,128)(2,1)} %shard_map.67), calls=%async_computation | async-start | bytes 1572864 | tf_op jit(solution)/shard_map/all_to_all | solution.py:253
  19.1 51.1 %collective-permute-start.5 = (bf16[250,4096]{1,0:T(8,128)(2,1)}, bf16[250,4096]{1,0:T(8,128)(2,1)}, u32[]{:S(2)}, u32[]{:S(2)}) collective-permute-start(bf16[250,4096]{1,0:T(8,128)(2,1)} %refs_2_.1), channel_id=1, source_target_pairs={{0,32},{32,0},{1,33},{33,1},{2,34},{34,2},{3,35},{35,3},{4,36},{36... | collective-permute-start | bytes 6144008 | tf_op jit(solution)/shard_map/ppermute | solution.py:257
  21.0 33.6 %collective-permute-start.4 = (bf16[250,2048]{1,0:T(8,128)(2,1)S(1)}, bf16[250,2048]{1,0:T(8,128)(2,1)S(1)}, u32[]{:S(2)}, u32[]{:S(2)}) collective-permute-start(bf16[250,2048]{1,0:T(8,128)(2,1)S(1)} %copy-done), channel_id=1, source_target_pairs={{0,32},{32,0},{1,33},{33,1},{2,34},{34,2},{3,35},{35,3},{4,36},{36... | collective-permute-start | bytes 3072008 | tf_op jit(solution)/shard_map/ppermute | solution.py:257
  44.0 12.9 %collective-permute-start = (bf16[768,256]{1,0:T(8,128)(2,1)S(1)}, bf16[768,256]{1,0:T(8,128)(2,1)S(1)}, u32[]{:S(2)}, u32[]{:S(2)}) collective-permute-start(bf16[768,256]{1,0:T(8,128)(2,1)S(1)} %get-tuple-element.17.refs_4_.refs_0_), channel_id=1, source_target_pairs={{0,1},{1,2},{2,3},{3,0},{4,5},{5,6},{6,7},{7,4},{8,9},{9,10},{10,1... | collective-permute-start | bytes 1179656 | tf_op jit(solution)/shard_map/ppermute | solution.py:261
  47.4 14.2 %collective-permute-start.2 = (bf16[768,256]{1,0:T(8,128)(2,1)}, bf16[768,256]{1,0:T(8,128)(2,1)S(1)}, u32[]{:S(2)}, u32[]{:S(2)}) collective-permute-start(bf16[768,256]{1,0:T(8,128)(2,1)} %get-tuple-element.18.refs_5_.refs_1_), channel_id=1, source_target_pairs={{0,3},{1,0},{2,1},{3,2},{4,7},{5,4},{6,5},{7,6},{8,11},{9,8},{10,9... | collective-permute-start | bytes 1179656 | tf_op jit(solution)/shard_map/ppermute | solution.py:261
  51.1 19.0 %collective-permute-start.6 = (bf16[768,256]{1,0:T(8,128)(2,1)S(1)}, bf16[768,256]{1,0:T(8,128)(2,1)}, u32[]{:S(2)}, u32[]{:S(2)}) collective-permute-start(bf16[768,256]{1,0:T(8,128)(2,1)S(1)} %get-tuple-element.17.refs_4_.refs_0_), channel_id=1, source_target_pairs={{0,3},{1,0},{2,1},{3,2},{4,7},{5,4},{6,5},{7,6},{8,11},{9,8},{10,9... | collective-permute-start | bytes 1179656 | tf_op jit(solution)/shard_map/ppermute | solution.py:261
  54.6 15.6 %collective-permute-start.7 = (bf16[768,256]{1,0:T(8,128)(2,1)}, bf16[768,256]{1,0:T(8,128)(2,1)}, u32[]{:S(2)}, u32[]{:S(2)}) collective-permute-start(bf16[768,256]{1,0:T(8,128)(2,1)} %get-tuple-element.18.refs_5_.refs_1_), channel_id=1, source_target_pairs={{0,1},{1,2},{2,3},{3,0},{4,5},{5,6},{6,7},{7,4},{8,9},{9,10},{10,1... | collective-permute-start | bytes 1179656 | tf_op jit(solution)/shard_map/ppermute | solution.py:261
  57.0 21.1 %collective-permute-start.1 = (bf16[768,256]{1,0:T(8,128)(2,1)S(1)}, bf16[768,256]{1,0:T(8,128)(2,1)}, u32[]{:S(2)}, u32[]{:S(2)}) collective-permute-start(bf16[768,256]{1,0:T(8,128)(2,1)S(1)} %collective-permute-done.refs_8_.refs_6_), channel_id=1, source_target_pairs={{0,1},{1,2},{2,3},{3,0},{4,5},{5,6},{6,7},{7,4},{8,9},{9,10},{10,1... | collective-permute-start | bytes 1179656 | tf_op jit(solution)/shard_map/ppermute | solution.py:261
  61.6 16.5 %collective-permute-start.3 = (bf16[768,256]{1,0:T(8,128)(2,1)S(1)}, bf16[768,256]{1,0:T(8,128)(2,1)}, u32[]{:S(2)}, u32[]{:S(2)}) collective-permute-start(bf16[768,256]{1,0:T(8,128)(2,1)S(1)} %collective-permute-done.2.refs_7_.refs_3_), channel_id=1, source_target_pairs={{0,3},{1,0},{2,1},{3,2},{4,7},{5,4},{6,5},{7,6},{8,11},{9,8},{10,9... | collective-permute-start | bytes 1179656 | tf_op jit(solution)/shard_map/ppermute | solution.py:261
  70.1 1.6 %copy-start.1 = (bf16[250,4096]{1,0:T(8,128)(2,1)S(1)}, bf16[250,4096]{1,0:T(8,128)(2,1)}, u32[]{:S(2)}) copy-start(bf16[250,4096]{1,0:T(8,128)(2,1)} %refs_2_.1) | copy-start | bytes 6144004
  108.8 1.0 copy-start.2
  109.8 14.7 %all-to-all-start.3 = ((bf16[8,256,256]{2,1,0:T(8,128)(2,1)}), bf16[8,256,256]{2,1,0:T(8,128)(2,1)S(1)}, u32[]{:S(2)}, u32[]{:S(2)}) async-start(bf16[8,256,256]{2,1,0:T(8,128)(2,1)} %copy-done.2), calls=%async_computation.3 | async-start | bytes 2097152 | tf_op jit(solution)/shard_map/all_to_all | solution.py:253
  116.4 12.9 %collective-permute-start.8 = (bf16[250,2176]{1,0:T(8,128)(2,1)S(1)}, bf16[250,2176]{1,0:T(8,128)(2,1)}, u32[]{:S(2)}, u32[]{:S(2)}) collective-permute-start(bf16[250,2176]{1,0:T(8,128)(2,1)S(1)} %shard_map.74._), channel_id=1, source_target_pairs={{0,32},{32,0},{1,33},{33,1},{2,34},{34,2},{3,35},{35,3},{4,36},{36... | collective-permute-start | bytes 3264008 | tf_op jit(solution)/shard_map/ppermute | solution.py:257
  124.7 0.6 copy-start.3
  125.4 16.2 %all-to-all-start.4 = ((bf16[32,16,128]{2,1,0:T(8,128)(2,1)}), bf16[32,16,128]{2,1,0:T(8,128)(2,1)S(1)}, u32[]{:S(2)}, u32[]{:S(2)}) async-start(bf16[32,16,128]{2,1,0:T(8,128)(2,1)} %copy-done.3), calls=%async_computation.4 | async-start | bytes 262144 | tf_op jit(solution)/shard_map/all_to_all | solution.py:253

commit v5 on v4

--- a/solution.py
+++ b/solution.py
@@ -351,7 +351,7 @@
     )
     sent = call(sent_kernel, array((rows, D_S + 128), BF), grads, full_s, kl, flops=2 * rows * ALL * D_S)
     packed = call(
-        pack_kernel, array((Z * YQ, HALF, 2 * FS), BF), exchange(by_ypx, ("yp", "x")), sent, anywhere=1
+        pack_kernel, array((Z * YQ, HALF, 2 * FS), BF), exchange(by_ypx, ("yp", "x")), sent, anywhere=1, mib=60
     )
     hidden_grad = call(last_kernel, array((TOK, FS), F32), exchange(packed, ("z", "yq")))
     head_grad, loss = call(

time: 143 us -> 145 us (1.014)
  Pallas kernels: 17.8 us -> 19.7 us
    pallas_call x11, Pallas kernels: 17.8 us -> 19.7 us  [call(): pl.pallas_call(kernel, out_shape=out, in_specs=specs, out_specs=outs, scr...]
  transfers between devices with their start and end apart: 12 -> 12, of which waited for: 5 -> 5; matrix products, arithmetic and copies ran while one was open for 0% -> 0% of each run, Pallas kernels for 9% -> 10%
where the time goes in v5:
time: 145 us; the launch traced here: 144 us
  starting transfers between devices  51.9 us (36%)
  waiting for transfers between devices  41.7 us (29%)
  blocking collectives  27.6 us (19%)
  Pallas kernels  19.7 us (14%)
  local copies, waits for them, and re-layouts  2.56 us (2%)
    all_to_all x3, waiting for transfers between devices, exchange(): return lax.all_to_all(v, axes, 0, 0, tiled=True)  35.6 us
    all_to_all x2, blocking collectives, exchange(): return lax.all_to_all(v, axes, 0, 0, tiled=True)  27.6 us
    all_to_all x3, starting transfers between devices, exchange(): return lax.all_to_all(v, axes, 0, 0, tiled=True)  25.8 us
    ppermute x6, starting transfers between devices, along_x(): return lax.ppermute(v, 'x', [(i, (i + step) % X) for i in range(X)])  19.9 us
    pallas_call x11, Pallas kernels, call(): pl.pallas_call(kernel, out_shape=out, in_specs=specs, out_specs=outs, scr...  19.7 us
    ppermute x3, starting transfers between devices, swap(): return lax.ppermute(v, 'core', [(0, 1), (1, 0)])  6.25 us
    ppermute x6, waiting for transfers between devices, along_x(): return lax.ppermute(v, 'x', [(i, (i + step) % X) for i in range(X)])  6.09 us
  transfers between devices with their start and end apart: 12, of which 5 were waited for; matrix products, arithmetic and copies ran while one was open for 0% of the time, Pallas kernels for 10%

profile of v5, /device:TPU:8, one launch (start us, length us, event | category | flops | bytes accessed | tf_op | source)
XLA Modules:
  0.0 144.3 jit_solution(13769826373328000083)
XLA Ops:
  0.6 0.0 copy-start.1
  0.6 1.8 %shard_map.67 = bf16[64,48,128]{2,1,0:T(8,128)(2,1)} custom-call(bf16[30,64]{1,0:T(8,128)(2,1)} %s_any.1, bf16[30,128]{1,0:T(8,128)(2,1)} %t_any.1), custom_call_target="tpu_custom_call" | custom-call | bytes 797952 | tf_op jit(solution)/shard_map/pallas_call | solution.py:34
  2.5 16.6 %all-to-all-start = ((bf16[64,48,128]{2,1,0:T(8,128)(2,1)}), bf16[64,48,128]{2,1,0:T(8,128)(2,1)S(1)}, u32[]{:S(2)}, u32[]{:S(2)}) async-start(bf16[64,48,128]{2,1,0:T(8,128)(2,1)} %shard_map.67), calls=%async_computation | async-start | bytes 1572864 | tf_op jit(solution)/shard_map/all_to_all | solution.py:253
  19.1 1.9 %collective-permute-start.5 = (bf16[250,4096]{1,0:T(8,128)(2,1)}, bf16[250,4096]{1,0:T(8,128)(2,1)}, u32[]{:S(2)}, u32[]{:S(2)}) collective-permute-start(bf16[250,4096]{1,0:T(8,128)(2,1)} %refs_2_.1), channel_id=1, source_target_pairs={{0,32},{32,0},{1,33},{33,1},{2,34},{34,2},{3,35},{35,3},{4,36},{36... | collective-permute-start | bytes 6144008 | tf_op jit(solution)/shard_map/ppermute | solution.py:257
  21.0 0.0 copy-done.1
  21.0 2.4 %collective-permute-start.4 = (bf16[250,2048]{1,0:T(8,128)(2,1)S(1)}, bf16[250,2048]{1,0:T(8,128)(2,1)S(1)}, u32[]{:S(2)}, u32[]{:S(2)}) collective-permute-start(bf16[250,2048]{1,0:T(8,128)(2,1)S(1)} %copy-done.1), channel_id=1, source_target_pairs={{0,32},{32,0},{1,33},{33,1},{2,34},{34,2},{3,35},{35,3},{4,36},{36... | collective-permute-start | bytes 3072008 | tf_op jit(solution)/shard_map/ppermute | solution.py:257
  23.4 19.6 %all-to-all-done = bf16[64,48,128]{2,1,0:T(8,128)(2,1)S(1)} async-done(((bf16[64,48,128]{2,1,0:T(8,128)(2,1)}), bf16[64,48,128]{2,1,0:T(8,128)(2,1)S(1)}, u32[]{:S(2)}, u32[]{:S(2)}) %all-to-all-start) | async-done | bytes 786464 | tf_op jit(solution)/shard_map/all_to_all | solution.py:253
  43.0 1.0 shard_map.68
  44.1 3.4 %collective-permute-start = (bf16[768,256]{1,0:T(8,128)(2,1)S(1)}, bf16[768,256]{1,0:T(8,128)(2,1)S(1)}, u32[]{:S(2)}, u32[]{:S(2)}) collective-permute-start(bf16[768,256]{1,0:T(8,128)(2,1)S(1)} %get-tuple-element.17.refs_4_.refs_0_), channel_id=1, source_target_pairs={{0,1},{1,2},{2,3},{3,0},{4,5},{5,6},{6,7},{7,4},{8,9},{9,10},{10,1... | collective-permute-start | bytes 1179656 | tf_op jit(solution)/shard_map/ppermute | solution.py:261
  47.4 3.7 %collective-permute-start.2 = (bf16[768,256]{1,0:T(8,128)(2,1)}, bf16[768,256]{1,0:T(8,128)(2,1)S(1)}, u32[]{:S(2)}, u32[]{:S(2)}) collective-permute-start(bf16[768,256]{1,0:T(8,128)(2,1)} %get-tuple-element.18.refs_5_.refs_1_), channel_id=1, source_target_pairs={{0,3},{1,0},{2,1},{3,2},{4,7},{5,4},{6,5},{7,6},{8,11},{9,8},{10,9... | collective-permute-start | bytes 1179656 | tf_op jit(solution)/shard_map/ppermute | solution.py:261
  51.1 3.5 %collective-permute-start.6 = (bf16[768,256]{1,0:T(8,128)(2,1)S(1)}, bf16[768,256]{1,0:T(8,128)(2,1)}, u32[]{:S(2)}, u32[]{:S(2)}) collective-permute-start(bf16[768,256]{1,0:T(8,128)(2,1)S(1)} %get-tuple-element.17.refs_4_.refs_0_), channel_id=1, source_target_pairs={{0,3},{1,0},{2,1},{3,2},{4,7},{5,4},{6,5},{7,6},{8,11},{9,8},{10,9... | collective-permute-start | bytes 1179656 | tf_op jit(solution)/shard_map/ppermute | solution.py:261
  54.6 0.0 collective-permute-done.4.refs_1_.s1_ref
  54.6 2.4 %collective-permute-start.7 = (bf16[768,256]{1,0:T(8,128)(2,1)}, bf16[768,256]{1,0:T(8,128)(2,1)}, u32[]{:S(2)}, u32[]{:S(2)}) collective-permute-start(bf16[768,256]{1,0:T(8,128)(2,1)} %get-tuple-element.18.refs_5_.refs_1_), channel_id=1, source_target_pairs={{0,1},{1,2},{2,3},{3,0},{4,5},{5,6},{6,7},{7,4},{8,9},{9,10},{10,1... | collective-permute-start | bytes 1179656 | tf_op jit(solution)/shard_map/ppermute | solution.py:261
  57.0 0.0 collective-permute-done.refs_8_.refs_6_
  57.0 2.2 %collective-permute-start.1 = (bf16[768,256]{1,0:T(8,128)(2,1)S(1)}, bf16[768,256]{1,0:T(8,128)(2,1)}, u32[]{:S(2)}, u32[]{:S(2)}) collective-permute-start(bf16[768,256]{1,0:T(8,128)(2,1)S(1)} %collective-permute-done.refs_8_.refs_6_), channel_id=1, source_target_pairs={{0,1},{1,2},{2,3},{3,0},{4,5},{5,6},{6,7},{7,4},{8,9},{9,10},{10,1... | collective-permute-start | bytes 1179656 | tf_op jit(solution)/shard_map/ppermute | solution.py:261
  59.2 2.4 %collective-permute-done.2.refs_7_.refs_3_ = bf16[768,256]{1,0:T(8,128)(2,1)S(1)} collective-permute-done((bf16[768,256]{1,0:T(8,128)(2,1)}, bf16[768,256]{1,0:T(8,128)(2,1)S(1)}, u32[]{:S(2)}, u32[]{:S(2)}) %collective-permute-start.2) | collective-permute-done | bytes 393248 | tf_op jit(solution)/shard_map/ppermute | solution.py:261
  61.6 4.9 %collective-permute-start.3 = (bf16[768,256]{1,0:T(8,128)(2,1)S(1)}, bf16[768,256]{1,0:T(8,128)(2,1)}, u32[]{:S(2)}, u32[]{:S(2)}) collective-permute-start(bf16[768,256]{1,0:T(8,128)(2,1)S(1)} %collective-permute-done.2.refs_7_.refs_3_), channel_id=1, source_target_pairs={{0,3},{1,0},{2,1},{3,2},{4,7},{5,4},{6,5},{7,6},{8,11},{9,8},{10,9... | collective-permute-start | bytes 1179656 | tf_op jit(solution)/shard_map/ppermute | solution.py:261
  66.5 3.7 %collective-permute-done.6.refs_6_.refs_2_ = bf16[768,256]{1,0:T(8,128)(2,1)} collective-permute-done((bf16[768,256]{1,0:T(8,128)(2,1)S(1)}, bf16[768,256]{1,0:T(8,128)(2,1)}, u32[]{:S(2)}, u32[]{:S(2)}) %collective-permute-start.6) | collective-permute-done | bytes 393248 | tf_op jit(solution)/shard_map/ppermute | solution.py:261
  70.1 0.0 collective-permute-done.7.refs_9_.refs_7_
  70.1 0.0 collective-permute-done.5.refs_3_
  70.1 0.0 copy-start.2
  70.1 1.6 %copy-done.2 = bf16[250,4096]{1,0:T(8,128)(2,1)S(1)} copy-done((bf16[250,4096]{1,0:T(8,128)(2,1)S(1)}, bf16[250,4096]{1,0:T(8,128)(2,1)}, u32[]{:S(2)}) %copy-start.2) | copy-done | bytes 2048024
  71.7 6.4 %shard_map.69 = (f32[2,250,256]{2,1,0:T(8,128)S(1)}, f32[2,250,256]{2,1,0:T(8,128)S(1)}, bf16[2,250,1024]{2,1,0:T(8,128)(2,1)S(1)}, bf16[2,250,1024]{2,1,0:T(8,128)(2,1)S(1)}) custom-call(s32[1]{0:T(128)} %bitcast.x_ref, bf16[250,2048]{1,0:T(8,128)(2,1)S(1)} %copy-done.1, bf16[250,2048]{1,0:T(8,128)(2,1)S(1)} %collective-permute-done.4.refs_1_.s1_ref, ...), custom_call_target="tpu_custom_call" | custom-call | tf_op jit(solution)/shard_map/pallas_call | solution.py:34
  78.1 0.0 collective-permute-done.1.lo_ref.refs_4_
  78.1 0.0 collective-permute-done.3.hi_ref.refs_5_
  78.1 2.2 %shard_map.70 = (f32[2,250,256]{2,1,0:T(8,128)S(1)}, f32[2,250,256]{2,1,0:T(8,128)S(1)}, f32[32,8,128]{2,1,0:T(8,128)S(1)}) custom-call(s32[1]{0:T(128)} %bitcast.x_ref, bf16[768,256]{1,0:T(8,128)(2,1)} %collective-permute-done.1.lo_ref.refs_4_, bf16[768,256]{1,0:T(8,128)(2,1)} %collective-permute-done.3.hi_ref.refs_5_, ...), custom_call_target="tpu_custom_call" | custom-call | flops 524288000 | bytes 5013508 | tf_op jit(solution)/shard_map/pallas_call | solution.py:34
  80.3 17.2 %all_to_all.25.p_ref = f32[32,8,128]{2,1,0:T(8,128)S(1)} all-to-all(f32[32,8,128]{2,1,0:T(8,128)S(1)} %get-tuple-element.23), channel_id=1, replica_groups=mesh['z'=8,'core'=2,'yq'=4,'yp'=2,'x'=4] {'yq','yp','x'}, dimensions={0} | all-to-all | bytes 262144 | tf_op jit(solution)/shard_map/all_to_all | solution.py:253
  97.5 0.1 shard_map.71
  97.6 10.4 %all_to_all.26.p_ref = f32[8,8,128]{2,1,0:T(8,128)S(1)} all-to-all(f32[8,8,128]{2,1,0:T(8,128)S(1)} %shard_map.71), channel_id=1, replica_groups=mesh['z'=8,'core'=2,'yq'=4,'yp'=2,'x'=4] {'z'}, dimensions={0} | all-to-all | bytes 65536 | tf_op jit(solution)/shard_map/all_to_all | solution.py:253
  107.9 0.9 shard_map.72
  108.9 0.0 copy-start.3
  108.9 1.0 copy-done.3
  109.8 5.3 %all-to-all-start.3 = ((bf16[8,256,256]{2,1,0:T(8,128)(2,1)}), bf16[8,256,256]{2,1,0:T(8,128)(2,1)}, u32[]{:S(2)}, u32[]{:S(2)}) async-start(bf16[8,256,256]{2,1,0:T(8,128)(2,1)} %copy-done.3), calls=%async_computation.3 | async-start | bytes 2097152 | tf_op jit(solution)/shard_map/all_to_all | solution.py:253
  115.2 1.4 shard_map.73.full_s
  116.6 0.5 shard_map.74._
  117.1 0.0 copy-start
  117.1 1.9 %collective-permute-start.8 = (bf16[250,2176]{1,0:T(8,128)(2,1)S(1)}, bf16[250,2176]{1,0:T(8,128)(2,1)}, u32[]{:S(2)}, u32[]{:S(2)}) collective-permute-start(bf16[250,2176]{1,0:T(8,128)(2,1)S(1)} %shard_map.74._), channel_id=1, source_target_pairs={{0,32},{32,0},{1,33},{33,1},{2,34},{34,2},{3,35},{35,3},{4,36},{36... | collective-permute-start | bytes 3264008 | tf_op jit(solution)/shard_map/ppermute | solution.py:257
  119.0 6.3 %all-to-all-done.3.r_ref = bf16[8,256,256]{2,1,0:T(8,128)(2,1)} async-done(((bf16[8,256,256]{2,1,0:T(8,128)(2,1)}), bf16[8,256,256]{2,1,0:T(8,128)(2,1)}, u32[]{:S(2)}, u32[]{:S(2)}) %all-to-all-start.3) | async-done | bytes 1048608 | tf_op jit(solution)/shard_map/all_to_all | solution.py:253
  125.3 0.0 copy-done
  125.3 2.1 %shard_map.76 = bf16[32,16,128]{2,1,0:T(8,128)(2,1)} custom-call(bf16[8,256,256]{2,1,0:T(8,128)(2,1)} %all-to-all-done.3.r_ref, bf16[250,2176]{1,0:T(8,128)(2,1)} %copy-done), custom_call_target="tpu_custom_call" | custom-call | bytes 2267648 | tf_op jit(solution)/shard_map/pallas_call | solution.py:34
  127.4 3.8 %all-to-all-start.4 = ((bf16[32,16,128]{2,1,0:T(8,128)(2,1)}), bf16[32,16,128]{2,1,0:T(8,128)(2,1)S(1)}, u32[]{:S(2)}, u32[]{:S(2)}) async-start(bf16[32,16,128]{2,1,0:T(8,128)(2,1)} %shard_map.76), calls=%async_computation.4 | async-start | bytes 262144 | tf_op jit(solution)/shard_map/all_to_all | solution.py:253
  131.2 0.0 collective-permute-done.8.arrived
  131.2 2.7 %shard_map.75 = (bf16[250,2048]{1,0:T(8,128)(2,1)}, f32[1,1]{1,0:T(1,128)}) custom-call(bf16[2,250,256]{2,1,0:T(8,128)(2,1)S(1)} %get-tuple-element.26.g_ref, bf16[2048,256]{1,0:T(8,128)(2,1)S(1)} %shard_map.73.full_s, f32[8,128]{1,0:T(8,128)S(1)} %get-tuple-element.27.refs_8_.kl_ref, bf16[250,2176]{1,0:T(8,128)(2,1)} %collective-permute-done.8.arrived), custom_call_target="tpu_custom_call" | custom-call | flops 262144000 | bytes 3420676 | tf_op jit(solution)/shard_map/pallas_call | solution.py:34
  133.9 9.7 %all-to-all-done.4.r_ref = bf16[32,16,128]{2,1,0:T(8,128)(2,1)S(1)} async-done(((bf16[32,16,128]{2,1,0:T(8,128)(2,1)}), bf16[32,16,128]{2,1,0:T(8,128)(2,1)S(1)}, u32[]{:S(2)}, u32[]{:S(2)}) %all-to-all-start.4) | async-done | bytes 131104 | tf_op jit(solution)/shard_map/all_to_all | solution.py:253
  143.6 0.7 shard_map.77
Async XLA Ops:
  0.6 20.4 %copy-start.1 = (bf16[250,2048]{1,0:T(8,128)(2,1)S(1)}, bf16[250,2048]{1,0:T(8,128)(2,1)}, u32[]{:S(2)}) copy-start(bf16[250,2048]{1,0:T(8,128)(2,1)} %s0_ref.1) | copy-start | bytes 3072004
  2.5 40.6 %all-to-all-start = ((bf16[64,48,128]{2,1,0:T(8,128)(2,1)}), bf16[64,48,128]{2,1,0:T(8,128)(2,1)S(1)}, u32[]{:S(2)}, u32[]{:S(2)}) async-start(bf16[64,48,128]{2,1,0:T(8,128)(2,1)} %shard_map.67), calls=%async_computation | async-start | bytes 1572864 | tf_op jit(solution)/shard_map/all_to_all | solution.py:253
  19.1 51.1 %collective-permute-start.5 = (bf16[250,4096]{1,0:T(8,128)(2,1)}, bf16[250,4096]{1,0:T(8,128)(2,1)}, u32[]{:S(2)}, u32[]{:S(2)}) collective-permute-start(bf16[250,4096]{1,0:T(8,128)(2,1)} %refs_2_.1), channel_id=1, source_target_pairs={{0,32},{32,0},{1,33},{33,1},{2,34},{34,2},{3,35},{35,3},{4,36},{36... | collective-permute-start | bytes 6144008 | tf_op jit(solution)/shard_map/ppermute | solution.py:257
  21.0 33.6 %collective-permute-start.4 = (bf16[250,2048]{1,0:T(8,128)(2,1)S(1)}, bf16[250,2048]{1,0:T(8,128)(2,1)S(1)}, u32[]{:S(2)}, u32[]{:S(2)}) collective-permute-start(bf16[250,2048]{1,0:T(8,128)(2,1)S(1)} %copy-done.1), channel_id=1, source_target_pairs={{0,32},{32,0},{1,33},{33,1},{2,34},{34,2},{3,35},{35,3},{4,36},{36... | collective-permute-start | bytes 3072008 | tf_op jit(solution)/shard_map/ppermute | solution.py:257
  44.1 12.9 %collective-permute-start = (bf16[768,256]{1,0:T(8,128)(2,1)S(1)}, bf16[768,256]{1,0:T(8,128)(2,1)S(1)}, u32[]{:S(2)}, u32[]{:S(2)}) collective-permute-start(bf16[768,256]{1,0:T(8,128)(2,1)S(1)} %get-tuple-element.17.refs_4_.refs_0_), channel_id=1, source_target_pairs={{0,1},{1,2},{2,3},{3,0},{4,5},{5,6},{6,7},{7,4},{8,9},{9,10},{10,1... | collective-permute-start | bytes 1179656 | tf_op jit(solution)/shard_map/ppermute | solution.py:261
  47.4 14.2 %collective-permute-start.2 = (bf16[768,256]{1,0:T(8,128)(2,1)}, bf16[768,256]{1,0:T(8,128)(2,1)S(1)}, u32[]{:S(2)}, u32[]{:S(2)}) collective-permute-start(bf16[768,256]{1,0:T(8,128)(2,1)} %get-tuple-element.18.refs_5_.refs_1_), channel_id=1, source_target_pairs={{0,3},{1,0},{2,1},{3,2},{4,7},{5,4},{6,5},{7,6},{8,11},{9,8},{10,9... | collective-permute-start | bytes 1179656 | tf_op jit(solution)/shard_map/ppermute | solution.py:261
  51.1 19.0 %collective-permute-start.6 = (bf16[768,256]{1,0:T(8,128)(2,1)S(1)}, bf16[768,256]{1,0:T(8,128)(2,1)}, u32[]{:S(2)}, u32[]{:S(2)}) collective-permute-start(bf16[768,256]{1,0:T(8,128)(2,1)S(1)} %get-tuple-element.17.refs_4_.refs_0_), channel_id=1, source_target_pairs={{0,3},{1,0},{2,1},{3,2},{4,7},{5,4},{6,5},{7,6},{8,11},{9,8},{10,9... | collective-permute-start | bytes 1179656 | tf_op jit(solution)/shard_map/ppermute | solution.py:261
  54.6 15.6 %collective-permute-start.7 = (bf16[768,256]{1,0:T(8,128)(2,1)}, bf16[768,256]{1,0:T(8,128)(2,1)}, u32[]{:S(2)}, u32[]{:S(2)}) collective-permute-start(bf16[768,256]{1,0:T(8,128)(2,1)} %get-tuple-element.18.refs_5_.refs_1_), channel_id=1, source_target_pairs={{0,1},{1,2},{2,3},{3,0},{4,5},{5,6},{6,7},{7,4},{8,9},{9,10},{10,1... | collective-permute-start | bytes 1179656 | tf_op jit(solution)/shard_map/ppermute | solution.py:261
  57.0 21.1 %collective-permute-start.1 = (bf16[768,256]{1,0:T(8,128)(2,1)S(1)}, bf16[768,256]{1,0:T(8,128)(2,1)}, u32[]{:S(2)}, u32[]{:S(2)}) collective-permute-start(bf16[768,256]{1,0:T(8,128)(2,1)S(1)} %collective-permute-done.refs_8_.refs_6_), channel_id=1, source_target_pairs={{0,1},{1,2},{2,3},{3,0},{4,5},{5,6},{6,7},{7,4},{8,9},{9,10},{10,1... | collective-permute-start | bytes 1179656 | tf_op jit(solution)/shard_map/ppermute | solution.py:261
  61.6 16.5 %collective-permute-start.3 = (bf16[768,256]{1,0:T(8,128)(2,1)S(1)}, bf16[768,256]{1,0:T(8,128)(2,1)}, u32[]{:S(2)}, u32[]{:S(2)}) collective-permute-start(bf16[768,256]{1,0:T(8,128)(2,1)S(1)} %collective-permute-done.2.refs_7_.refs_3_), channel_id=1, source_target_pairs={{0,3},{1,0},{2,1},{3,2},{4,7},{5,4},{6,5},{7,6},{8,11},{9,8},{10,9... | collective-permute-start | bytes 1179656 | tf_op jit(solution)/shard_map/ppermute | solution.py:261
  70.1 1.6 %copy-start.2 = (bf16[250,4096]{1,0:T(8,128)(2,1)S(1)}, bf16[250,4096]{1,0:T(8,128)(2,1)}, u32[]{:S(2)}) copy-start(bf16[250,4096]{1,0:T(8,128)(2,1)} %refs_2_.1) | copy-start | bytes 6144004
  108.9 1.0 copy-start.3
  109.8 15.5 %all-to-all-start.3 = ((bf16[8,256,256]{2,1,0:T(8,128)(2,1)}), bf16[8,256,256]{2,1,0:T(8,128)(2,1)}, u32[]{:S(2)}, u32[]{:S(2)}) async-start(bf16[8,256,256]{2,1,0:T(8,128)(2,1)} %copy-done.3), calls=%async_computation.3 | async-start | bytes 2097152 | tf_op jit(solution)/shard_map/all_to_all | solution.py:253
  117.1 8.3 %copy-start = (bf16[250,2176]{1,0:T(8,128)(2,1)}, bf16[250,2176]{1,0:T(8,128)(2,1)S(1)}, u32[]{:S(2)}) copy-start(bf16[250,2176]{1,0:T(8,128)(2,1)S(1)} %shard_map.74._) | copy-start | bytes 3264004
  117.1 14.2 %collective-permute-start.8 = (bf16[250,2176]{1,0:T(8,128)(2,1)S(1)}, bf16[250,2176]{1,0:T(8,128)(2,1)}, u32[]{:S(2)}, u32[]{:S(2)}) collective-permute-start(bf16[250,2176]{1,0:T(8,128)(2,1)S(1)} %shard_map.74._), channel_id=1, source_target_pairs={{0,32},{32,0},{1,33},{33,1},{2,34},{34,2},{3,35},{35,3},{4,36},{36... | collective-permute-start | bytes 3264008 | tf_op jit(solution)/shard_map/ppermute | solution.py:257
  127.4 16.2 %all-to-all-start.4 = ((bf16[32,16,128]{2,1,0:T(8,128)(2,1)}), bf16[32,16,128]{2,1,0:T(8,128)(2,1)S(1)}, u32[]{:S(2)}, u32[]{:S(2)}) async-start(bf16[32,16,128]{2,1,0:T(8,128)(2,1)} %shard_map.76), calls=%async_computation.4 | async-start | bytes 262144 | tf_op jit(solution)/shard_map/all_to_all | solution.py:253
